TPU v7x, 128 devices: a whole 4x4x4 slice. The times are simulated.
128 devices in a mesh: seq: 4 (over x_hi, core), pair: 8 (over z, x_lo), dp: 4 (over y).
Axes of the slice: x: 4 (x_hi: 2, x_lo: 2; x = x_hi * 2 + x_lo), y: 4, z: 4, core: 2. Of those that a mesh axis runs over, the one named last changes fastest.
Arguments:
- features: bfloat16 [4, 8, 2048, 1536], P('dp', 'pair', 'seq'), may hold values from -6 to 6
- conv_weight: bfloat16 [5, 1536, 1536], P(None, 'pair'), may hold values from -0.0625 to 0.0625
- conv_bias: float32 [1536], replicated, may hold values from -3 to 3
- species_table: float32 [2, 1536], replicated, may hold values from -3 to 3
- species_id: int32 [4, 8], P('dp'), may hold values from 0 to 1
- norm_gain: float32 [1536], replicated, may hold values from 0.4 to 1.6
- qkv_weight: bfloat16 [3, 1536, 1536], P(None, ('pair', 'dp')), may hold values from -5 to 5
- out_weight: bfloat16 [1536, 1536], P(('pair', 'dp')), may hold values from -0.15625 to 0.15625
- left_weight: bfloat16 [1536, 128], replicated, may hold values from -0.15625 to 0.15625
- right_weight: bfloat16 [1536, 128], replicated, may hold values from -0.15625 to 0.15625
- mix_weight: bfloat16 [128, 128], replicated, may hold values from -0.5 to 0.5
Outputs:
- seq_out: bfloat16 [4, 8, 1024, 1536], P('dp', 'pair', 'seq')
- pair_map: bfloat16 [4, 8, 64, 64, 128], P('dp', None, 'seq', 'pair')
All inputs are finite; a program needn't handle non-finite values.
Results may differ from a plain program's by a relative error of at most 0.02.
Values may be sent and summed in bfloat16 or wider, within the bound.
A program may use at most 128 MiB of HBM per device.

v0:
```python
import math

import jax
import jax.numpy as jnp
from jax import lax
from jax.sharding import PartitionSpec as P

D = 1536
HEADS = 8
KW = 5
POOL = 16
SPECIES = 2


def extended(block, sides, width):
    for axis, dim in sides:
        count = lax.axis_size(axis)
        forward = [(i, i + 1) for i in range(count - 1)]
        backward = [(target, source) for source, target in forward]
        low = lax.ppermute(
            lax.slice_in_dim(block, block.shape[dim] - width, None, axis=dim), axis, forward
        )
        high = lax.ppermute(lax.slice_in_dim(block, 0, width, axis=dim), axis, backward)
        block = jnp.concatenate([low, block, high], axis=dim)
    return block


def rms_scale(values):
    return values * lax.rsqrt(jnp.mean(values * values, axis=-1, keepdims=True) + 1e-05)


def attend_heads(tokens, qkv_rows, norm_gain):
    head_dim = D // HEADS
    normed = (rms_scale(tokens.astype(jnp.float32)) * norm_gain).astype(jnp.bfloat16)
    query = jnp.einsum(
        "gwsd,ed->gwse", normed, qkv_rows[0], preferred_element_type=jnp.float32
    ).astype(jnp.bfloat16)
    local_kv = jnp.einsum(
        "gwsd,ked->kgwse", normed, qkv_rows[1:], preferred_element_type=jnp.float32
    ).astype(jnp.bfloat16)
    keys_vals = lax.all_gather(local_kv, "seq", axis=3, tiled=True)
    groups, windows, length, width = query.shape
    heads_here = width // head_dim
    total_keys = keys_vals.shape[3]
    query = query.reshape(groups, windows, length, heads_here, head_dim)
    keys = keys_vals[0].reshape(groups, windows, total_keys, heads_here, head_dim)
    values = keys_vals[1].reshape(groups, windows, total_keys, heads_here, head_dim)
    scores = jnp.einsum(
        "gwshe,gwkhe->gwhsk", query, keys, preferred_element_type=jnp.float32
    ) / math.sqrt(head_dim)
    weights = jax.nn.softmax(scores, axis=-1).astype(jnp.bfloat16)
    attended = jnp.einsum("gwhsk,gwkhe->gwshe", weights, values, preferred_element_type=jnp.float32)
    return attended.astype(jnp.bfloat16).reshape(groups, windows, length, width)


def local(
    features,
    conv_weight,
    conv_bias,
    species_table,
    species_id,
    norm_gain,
    qkv_weight,
    out_weight,
    left_weight,
    right_weight,
    mix_weight,
):
    pair_pos = lax.axis_index("pair")
    slim = conv_weight.shape[1]
    margin = KW // 2
    haloed = extended(features, (("seq", 2),), margin)
    chosen = (species_id[0][:, None] == jnp.arange(SPECIES, dtype=jnp.int32)[None, :]).astype(
        jnp.float32
    )
    species_rows = jnp.dot(chosen, species_table, precision=lax.Precision.HIGHEST)
    species_cols = lax.dynamic_slice_in_dim(species_rows, pair_pos * slim, slim, 1)
    bias_cols = lax.dynamic_slice_in_dim(conv_bias, pair_pos * slim, slim, 0)
    piece = lax.all_gather(haloed, "pair", axis=1, tiled=True)
    length = piece.shape[2] - 2 * margin
    total = jnp.zeros((piece.shape[0], piece.shape[1], length, slim), jnp.float32)
    for shift in range(KW):
        total = total + jnp.einsum(
            "gnrd,ed->gnre",
            piece[:, :, shift : shift + length],
            conv_weight[shift],
            preferred_element_type=jnp.float32,
        )
    active = jax.nn.gelu(total + bias_cols)
    pooled = jnp.max(active.reshape(piece.shape[0], piece.shape[1], length // 2, 2, slim), axis=3)
    sliced = (pooled + species_cols[None, :, None, :]).astype(jnp.bfloat16)
    own = lax.all_to_all(sliced, "pair", split_axis=1, concat_axis=3, tiled=True)
    qkv_full, out_full = (
        lax.all_gather(qkv_weight, ("pair", "dp"), axis=1, tiled=True),
        lax.all_gather(out_weight, ("pair", "dp"), axis=0, tiled=True),
    )
    attended = attend_heads(own, qkv_full, norm_gain)
    mixed = jnp.einsum("gwse,ed->gwsd", attended, out_full, preferred_element_type=jnp.float32)
    seq_out = (own.astype(jnp.float32) + mixed).astype(jnp.bfloat16)
    groups, windows, length, width = seq_out.shape
    rows = jnp.mean(
        seq_out.astype(jnp.float32).reshape(groups, windows, length // POOL, POOL, width), axis=3
    )
    unit = rms_scale(rows).astype(jnp.bfloat16)
    left = jnp.einsum(
        "gwid,dc->gwic", unit, left_weight, preferred_element_type=jnp.float32
    ).astype(jnp.bfloat16)
    right = jnp.einsum(
        "gwid,dc->gwic", unit, right_weight, preferred_element_type=jnp.float32
    ).astype(jnp.bfloat16)
    row_side = lax.all_gather(left, "pair", axis=1, tiled=True)[0]
    column_all = lax.all_gather(right, "seq", axis=2, tiled=True)
    column_side = lax.all_to_all(column_all, "pair", split_axis=2, concat_axis=1, tiled=True)[0]
    outer = row_side[:, :, None, :] * column_side[:, None, :, :]
    pair_map = jnp.einsum(
        "wijc,cd->wijd", outer, mix_weight, preferred_element_type=jnp.float32
    ).astype(jnp.bfloat16)
    return (seq_out, pair_map[None])


def solution(mesh):
    return jax.shard_map(
        local,
        mesh=mesh,
        in_specs=(
            P("dp", "pair", "seq", None),
            P(None, "pair", None),
            P(),
            P(),
            P("dp", None),
            P(),
            P(None, ("pair", "dp"), None),
            P(("pair", "dp"), None),
            P(),
            P(),
            P(),
        ),
        out_specs=(P("dp", "pair", "seq", None), P("dp", None, "seq", "pair", None)),
        check_vma=False,
    )
```

profile of v0, /device:TPU:1, one launch (start us, length us, event | category | flops | bytes accessed | tf_op | source)
XLA Modules:
  0.0 729.9 jit_solution(6994807671594837125)
XLA Ops:
  7.2 0.0 copy-start
  7.2 0.0 copy-start.8
  7.2 0.0 copy-start.7
  7.2 0.0 copy-start.6
  7.2 0.0 all-gather.7.cloned.1.call-start
  7.3 0.9 fusion.56
  8.2 6.2 collective-permute-start
  14.4 1.9 collective-permute-start.1
  16.3 0.0 collective-permute-done
  16.3 4.5 collective-permute-done.1
  20.8 2.9 pad_maximum_fusion
  23.7 0.0 all-gather.7.cloned.1.call-update
  23.8 0.0 all-gather.9.cloned.1.call-start
  23.8 0.7 all-gather.9.cloned.1.call-update
  24.5 0.0 all-gather.11.cloned.1.call-start
  24.6 0.8 dynamic_slice.6
  25.4 0.0 copy-done.7
  25.4 0.2 fusion.52
  25.6 0.1 constant_dynamic-slice_fusion
  25.6 248.4 %all-gather.7.cloned.1.call-done = bf16[1,8,516,1536]{3,2,0,1:T(8,128)(2,1)} async-done(((bf16[1,1,516,1536]{3,2,0,1:T(8,128)(2,1)}), bf16[1,8,516,1536]{3,2,0,1:T(8,128)(2,1)}) %all-gather.7.cloned.1.call-update) | async-done | bytes 12681232 | tf_op jit(solution)/shard_map/all_gather | solution.py:79
  274.0 10.7 %fusion.5 = f32[8,512,192]{1,2,0:T(8,128)} fusion(bf16[1,8,516,1536]{3,2,1,0:T(8,128)(2,1)} %bitcast.133, bf16[5,192,1536]{2,1,0:T(8,128)(2,1)S(1)} %copy-done.6), kind=kOutput, calls=%fused_computation.10 | convolution fusion | flops 2415919104 | bytes 16318464 | tf_op jit(solution)/shard_map/gnrd,ed->gnre/dot_general | solution.py:83
  284.7 0.0 copy-done.5
  284.7 5.7 fusion.4
  290.3 5.7 fusion.3
  296.0 5.6 fusion.2
  301.6 9.1 %fusion.20 = f32[8,512,192]{1,2,0:T(8,128)S(1)} fusion(f32[8,512,192]{1,2,0:T(8,128)} %fusion.2, f32[8,512,192]{1,2,0:T(8,128)} %fusion.3, f32[8,512,192]{1,2,0:T(8,128)} %fusion.5, f32[8,512,192]{1,2,0:T(8,128)} %fusion.4, bf16[1,8,516,1536]{3,2,1,0:T(8,128)(2,1)S(1)} %bitcast.137, f32[192]{0:T(256)S(1)} %dynamic_slice.6, bf16[5,192,1536]{2,1,0:T(8,128)(2,1)} %param.12), kind=kOutput, calls=%fused_computation.29 | convolution fusion | flops 2426142720 | bytes 28902400 | tf_op jit(solution)/shard_map/gnrd,ed->gnre/dot_general | solution.py:83
  310.7 3.5 copy.64
  314.2 2.9 bitcast_reduce_fusion
  317.2 0.2 fusion.29
  317.4 0.0 copy-start.4
  317.4 1.0 copy.65
  318.4 29.8 %all_to_all.8 = bf16[1,8,256,192]{2,3,0,1:T(8,128)(2,1)S(1)} all-to-all(bf16[1,8,256,192]{2,3,0,1:T(8,128)(2,1)S(1)} %copy.65), channel_id=1, replica_groups=mesh['seq'=4,'pair'=8,'dp'=4] {'pair'}, dimensions={1} | all-to-all | bytes 1572864 | tf_op jit(solution)/shard_map/all_to_all | solution.py:92
  348.2 0.2 multiply_reduce_fusion.1
  348.4 0.1 bitcast_convert_fusion
  348.6 103.2 %all-gather.9.cloned.1.call-done = bf16[3,1536,1536]{2,1,0:T(8,128)(2,1)} async-done(((bf16[3,48,1536]{2,1,0:T(8,128)(2,1)}), bf16[3,1536,1536]{2,1,0:T(8,128)(2,1)}) %all-gather.9.cloned.1.call-update) | async-done | bytes 14155792 | tf_op jit(solution)/shard_map/all_gather | solution.py:94
  451.7 0.0 copy-done.4
  451.7 7.8 %fusion.24 = bf16[2,1,1,256,1536]{4,3,0,2,1:T(8,128)(2,1)} fusion(bf16[3,1536,1536]{2,1,0:T(8,128)(2,1)} %all-gather.9.cloned.1.call-done, f32[256,1536]{0,1:T(8,128)S(1)} %bitcast.120, f32[1536]{0:T(1024)S(1)} %copy-done.4, f32[256]{0:T(256)S(1)} %add_rsqrt_fusion), kind=kOutput, calls=%fused_computation.31 | convolution fusion | flops 2417885184 | bytes 12590080 | tf_op jit(solution)/shard_map/gwsd,ked->kgwse/dot_general | solution.py:38
  459.5 0.0 all-gather.11.cloned.1.call-update
  459.5 0.0 all-gather.13.cloned.1.call-start
  459.6 0.5 all-gather.13.cloned.1.call-update
  460.1 0.1 mul.134
  460.2 1.7 copy.71
  461.9 0.3 multiply_convert_fusion
  462.1 3.8 fusion.28
  465.9 1.2 copy.69
  467.1 55.6 %all-gather.11.cloned.1.call-done = bf16[2,1,1,1024,1536]{4,3,0,2,1:T(8,128)(2,1)} async-done(((bf16[2,1,1,256,1536]{4,3,0,2,1:T(8,128)(2,1)}), bf16[2,1,1,1024,1536]{4,3,0,2,1:T(8,128)(2,1)}) %all-gather.11.cloned.1.call-update) | async-done | bytes 6291472 | tf_op jit(solution)/shard_map/all_gather | solution.py:41
  522.6 4.9 fusion.55
  527.5 4.7 copy.70
  532.3 2.9 copy.68
  535.2 8.4 %fusion.57 = (f32[8,256]{1,0:T(8,128)S(1)}, f32[8,256,1024]{2,1,0:T(8,128)}) fusion(bf16[256,8,192]{0,2,1:T(8,128)(2,1)} %bitcast.126, bf16[1024,8,192]{0,2,1:T(8,128)(2,1)} %bitcast.122), kind=kOutput, calls=%fused_computation.78 | convolution fusion | flops 811598848 | bytes 12328960 | tf_op jit(solution)/shard_map/sub | solution.py:51
  543.6 6.0 fusion.30
  549.5 114.6 %all-gather.13.cloned.1.call-done = bf16[1536,1536]{1,0:T(8,128)(2,1)} async-done(((bf16[48,1536]{1,0:T(8,128)(2,1)}), bf16[1536,1536]{1,0:T(8,128)(2,1)}) %all-gather.13.cloned.1.call-update) | async-done | bytes 4718608 | tf_op jit(solution)/shard_map/all_gather | solution.py:95
  664.2 5.5 convert_reduce_fusion
  669.7 0.1 multiply_reduce_fusion.2
  669.8 0.2 convolution_convert_fusion.2
  670.0 0.2 convolution_convert_fusion.1
  670.2 24.6 %all-gather.1 = bf16[64,128]{1,0:T(8,128)(2,1)S(1)} all-gather(bf16[16,128]{1,0:T(8,128)(2,1)S(1)} %convolution_convert_fusion.1), channel_id=3, replica_groups=mesh['seq'=4,'pair'=8,'dp'=4] {'seq'}, dimensions={0}, use_global_device_ids=true | all-gather | bytes 20480 | tf_op jit(solution)/shard_map/all_gather | solution.py:112
  694.9 0.5 broadcast.98
  695.4 0.7 reduce.11
  696.2 0.6 reshape.258
  696.8 3.3 all-to-all-start.1
  700.1 22.3 %all-gather = bf16[128,128]{1,0:T(8,128)(2,1)S(1)} all-gather(bf16[16,128]{1,0:T(8,128)(2,1)S(1)} %convolution_convert_fusion.2), channel_id=2, replica_groups=mesh['seq'=4,'pair'=8,'dp'=4] {'pair'}, dimensions={0}, use_global_device_ids=true | all-gather | bytes 36864 | tf_op jit(solution)/shard_map/all_gather | solution.py:111
  722.4 0.0 all-to-all-done.1
  722.4 0.9 fusion.31
  (15 shorter events, 0.1 us)
Async XLA Ops:
  7.2 662.6 %copy-start = (bf16[1536,128]{1,0:T(8,128)(2,1)S(1)}, bf16[1536,128]{1,0:T(8,128)(2,1)}, u32[]{:S(2)}) copy-start(bf16[1536,128]{1,0:T(8,128)(2,1)} %param.19) | copy-start | bytes 1179652
  7.2 18.2 %copy-start.8 = (s32[1,8]{1,0:T(1,128)S(1)}, s32[1,8]{1,0:T(1,128)}, u32[]{:S(2)}) copy-start(s32[1,8]{1,0:T(1,128)} %param.15) | copy-start | bytes 100
  7.2 18.2 %copy-start.7 = (f32[2,1536]{1,0:T(2,128)S(1)}, f32[2,1536]{1,0:T(2,128)}, u32[]{:S(2)}) copy-start(f32[2,1536]{1,0:T(2,128)} %param.14) | copy-start | bytes 36868
  7.2 266.8 %copy-start.6 = (bf16[5,192,1536]{2,1,0:T(8,128)(2,1)S(1)}, bf16[5,192,1536]{2,1,0:T(8,128)(2,1)}, u32[]{:S(2)}) copy-start(bf16[5,192,1536]{2,1,0:T(8,128)(2,1)} %param.12) | copy-start | bytes 8847364
  7.2 266.8 %all-gather.7.cloned.1.call-start = ((), (), s32[]{:S(2)}) async-start(), calls=%async_computation.2 | async-start | bytes 14376960 | tf_op jit(solution)/shard_map/all_gather | solution.py:79
  8.2 8.1 %collective-permute-start = (bf16[1,1,2,1536]{3,2,0,1:T(2,128)(2,1)S(1)}, bf16[1,1,2,1536]{3,2,0,1:T(2,128)(2,1)S(1)}, u32[]{:S(2)}, u32[]{:S(2)}) collective-permute-start(bf16[1,1,2,1536]{3,2,0,1:T(2,128)(2,1)S(1)} %get-tuple-element.4), channel_id=1, source_target_pairs={{0,32},{32,64},{64,96},{1,33},{33,65},{65,97},{2,34},{34,66},{66,9... | collective-permute-start | bytes 18440 | tf_op jit(solution)/shard_map/ppermute | solution.py:20
  14.4 6.5 collective-permute-start.1
  23.8 428.0 %all-gather.9.cloned.1.call-start = ((), (), s32[]{:S(2)}) async-start(), calls=%async_computation.3 | async-start | bytes 14598144 | tf_op jit(solution)/shard_map/all_gather | solution.py:94
  24.5 498.1 %all-gather.11.cloned.1.call-start = ((), (), s32[]{:S(2)}) async-start(), calls=%async_computation.4 | async-start | bytes 7864320 | tf_op jit(solution)/shard_map/all_gather | solution.py:41
  274.0 10.7 %copy-start.5 = (bf16[1,8,516,1536]{3,2,0,1:T(8,128)(2,1)S(1)}, bf16[1,8,516,1536]{3,2,0,1:T(8,128)(2,1)}, u32[]{:S(2)}) copy-start(bf16[1,8,516,1536]{3,2,0,1:T(8,128)(2,1)} %all-gather.7.cloned.1.call-done) | copy-start | bytes 38043652
  317.4 134.4 %copy-start.4 = (f32[1536]{0:T(1024)S(1)}, f32[1536]{0:T(1024)}, u32[]{:S(2)}) copy-start(f32[1536]{0:T(1024)} %param.16) | copy-start | bytes 18436
  459.5 204.6 %all-gather.13.cloned.1.call-start = ((), (), s32[]{:S(2)}) async-start(), calls=%async_computation.5 | async-start | bytes 4866048 | tf_op jit(solution)/shard_map/all_gather | solution.py:95
  535.2 8.4 %copy-start.1 = (bf16[1,1,1,1024,1536]{3,4,2,1,0:T(8,128)(2,1)S(1)}, bf16[1,1,1,1024,1536]{3,4,2,1,0:T(8,128)(2,1)}, u32[]{:S(2)}) copy-start(bf16[1,1,1,1024,1536]{3,4,2,1,0:T(8,128)(2,1)} %copy.68) | copy-start | bytes 9437188
  664.2 5.9 copy-start.2
  664.2 58.2 %copy-start.3 = (bf16[128,128]{1,0:T(8,128)(2,1)S(1)}, bf16[128,128]{1,0:T(8,128)(2,1)}, u32[]{:S(2)}) copy-start(bf16[128,128]{1,0:T(8,128)(2,1)} %param.21) | copy-start | bytes 98308
  696.8 25.6 %all-to-all-start.1 = ((bf16[8,2,512]{2,1,0:T(2,128)(2,1)}), bf16[8,2,512]{2,1,0:T(2,128)(2,1)S(1)}, u32[]{:S(2)}, u32[]{:S(2)}) async-start(bf16[8,2,512]{2,1,0:T(2,128)(2,1)} %reshape.258), calls=%async_computation.1 | async-start | bytes 32768 | tf_op jit(solution)/shard_map/all_to_all | solution.py:113
Sparse Core Ops, SparseCore 0:
  23.9 250.0 all-gather.6
  275.6 176.0 all-gather.8
  459.7 62.9 all-gather.10
  524.1 139.9 all-gather.12
where the time goes:
time: 736 us; the launch traced here: 730 us
  waiting for transfers between devices  527 us (72%)
  blocking collectives  76.6 us (10%)
  matrix products  69.7 us (9%)
  local copies, waits for them, and re-layouts  23 us (3%)
  between operations  14 us (2%)
  starting transfers between devices  11.6 us (2%)
  other arithmetic  7.57 us (1%)
    all_gather x1, waiting for transfers between devices, local(): piece = lax.all_gather(haloed, 'pair', axis=1, tiled=True)  248 us
    all_gather x1, waiting for transfers between devices, local(): lax.all_gather(out_weight, ('pair', 'dp'), axis=0, tiled=True)  115 us
    all_gather x1, waiting for transfers between devices, local(): lax.all_gather(qkv_weight, ('pair', 'dp'), axis=1, tiled=True)  103 us
    all_gather x1, waiting for transfers between devices, attend_heads(): keys_vals = lax.all_gather(local_kv, 'seq', axis=3, tiled=True)  55.6 us
    dot_general x5, matrix products, local(): jnp.einsum('gnrd,ed->gnre', piece[:, :, shift:shift + length], conv_weigh...  36.7 us
    all_to_all x1, blocking collectives, local(): lax.all_to_all(sliced, 'pair', split_axis=1, concat_axis=3, tiled=True)  29.8 us
    all_gather x1, blocking collectives, local(): column_all = lax.all_gather(right, 'seq', axis=2, tiled=True)  24.6 us
    all_gather x1, blocking collectives, local(): row_side = lax.all_gather(left, 'pair', axis=1, tiled=True)[0]  22.3 us
  transfers between devices with their start and end apart: 7, of which 5 were waited for; matrix products, arithmetic and copies ran while one was open for 11% of the time, Pallas kernels for 0%

commit v1 on v0

v1 whole, which is shorter than its diff:
```python
import math

import jax
import jax.numpy as jnp
from jax import lax
from jax.experimental import pallas as pl
from jax.experimental.pallas import tpu as pltpu
from jax.sharding import PartitionSpec as P

D = 1536
HEAD = 192
POOL = 16
SPECIES = 2
MESH = pl.DeviceIdType.MESH
BF = jnp.bfloat16
F32 = jnp.float32
HALF = 768
ROWS = 1120


def coords():
    s, p, y = lax.axis_index("seq"), lax.axis_index("pair"), lax.axis_index("dp")
    hi, c = lax.div(s, 2), lax.rem(s, 2)
    z, lo = lax.div(p, 2), lax.rem(p, 2)
    return s, p, y, hi, c, z, lo, 2 * hi + lo


def dev(x, y, z, c):
    return (2 * lax.div(x, 2) + c, 2 * z + lax.rem(x, 2), y)


def m4(v):
    return lax.rem(v + 4, 4)


def nt(a, b):
    return lax.dot_general(a, b, (((1,), (1,)), ((), ())), preferred_element_type=F32)


def nn(a, b):
    return lax.dot_general(a, b, (((1,), (0,)), ((), ())), preferred_element_type=F32)


def al(v, n):
    return pl.multiple_of(v, n)


class Sites:
    def __init__(self, ss, rs):
        self.ss, self.rs, self.n, self.all = ss, rs, 0, []

    def make(self, src, dst, device, pend=True):
        k = self.n
        self.n += 1
        cp = pltpu.make_async_remote_copy(
            src_ref=src, dst_ref=dst, send_sem=self.ss.at[k], recv_sem=self.rs.at[k],
            device_id=device, device_id_type=MESH,
        )
        if pend:
            self.all.append(cp)
        return cp

    def go(self, src, dst, device):
        cp = self.make(src, dst, device)
        cp.start()
        return cp


N_SITES = 128


def main_kernel(
    feat, cw_in, qkv_in, out_in, vec, lw, rw,
    seq_out, left_out, right_out,
    F, CW, acc, QT, AW, OW, TH, TA, TOK, NM, QH, AO, AT,
    ss, rs, ls,
):
    s, p, y, hi, c, z, lo, x = coords()
    xp, xm, x2 = m4(x + 1), m4(x - 1), m4(x + 2)
    sib = dev(x, y, z, 1 - c)
    st = Sites(ss, rs)

    barrier = pltpu.get_barrier_semaphore()
    peers = [sib]
    for xx in (xp, xm, x2):
        peers += [dev(xx, y, z, c), dev(xx, y, z, 1 - c)]
    for d in (1, -1):
        peers += [dev(x, m4(y + d), z, c), dev(x, y, m4(z + d), c)]
    for t in peers:
        pl.semaphore_signal(barrier, inc=1, device_id=t, device_id_type=MESH)

    lcopies = []

    def local(src, dst):
        cp = pltpu.make_async_copy(src, dst, ls.at[len(lcopies)])
        cp.start()
        lcopies.append(cp)
        return cp

    cols = pl.ds(al(c * HALF, 128), HALF)
    own_q = local(qkv_in, QT)
    own_f = local(feat, F.at[pl.ds(16, 512)])
    own_o = local(out_in.at[:, cols], OW.at[lo, z, y, :, cols])
    own_w = local(cw_in, CW.at[:, pl.ds(al(z * HEAD, 16), HEAD)])
    pl.semaphore_wait(barrier, len(peers))

    sgn = 1 - 2 * lax.rem(y + c, 2)
    zd, zs, zo = m4(z + sgn), m4(z - sgn), m4(z + 2)
    g = lax.rem(y + c, 2)
    r0 = c * 96
    to_z = dev(x, y, zd, c)

    def rows_of(slot, off, n):
        return pl.ds(al(slot * HEAD + r0 + off, 16), n)

    zA, zB, yA, yC, sb = {}, {}, {}, {}, {}

    def start_zA(t):
        zA[t] = st.go(cw_in.at[t, pl.ds(al(r0, 16), 96)], CW.at[t, rows_of(z, 0, 96)], to_z)

    def same(ref, device):
        return st.go(ref, ref, device)

    def pass_zA(t):
        zA[t].wait_recv()
        zB[t] = same(CW.at[t, rows_of(zs, 48 * g, 48)], to_z)
        yA[t] = [
            same(CW.at[t, rows_of(zs, 0, 48)], dev(x, m4(y + 1), z, c)),
            same(CW.at[t, rows_of(zs, 48, 48)], dev(x, m4(y - 1), z, c)),
        ]
        sb[t] = [same(CW.at[t, rows_of(zs, 0, 96)], sib)]

    def pass_zB(t):
        zB[t].wait_recv()
        yC[t] = same(CW.at[t, rows_of(zo, 48 * g, 48)], dev(x, m4(y + 1 - 2 * c), z, c))
        for cp in yA[t]:
            cp.wait_recv()
        sb[t].append(same(CW.at[t, rows_of(zd, 0, 96)], sib))

    def pass_yC(t):
        yC[t].wait_recv()
        sb[t].append(same(CW.at[t, rows_of(zo, 0, 96)], sib))

    start_zA(0)

    lastr, firstr = feat.at[pl.ds(496, 16)], feat.at[pl.ds(0, 16)]
    xn = m4(x + 2 * c)
    xq = m4(x + 2 * (1 - c))
    halo = [
        st.go(lastr, F.at[pl.ds(0, 16)], dev(xn, y, z, 1 - c)),
        st.go(firstr, F.at[pl.ds(528, 16)], dev(xq, y, z, 1 - c)),
        st.go(lastr, F.at[pl.ds(544, 16)], dev(m4(xn + 1), y, z, 1 - c)),
        st.go(firstr, F.at[pl.ds(1104, 16)], dev(m4(xq - 1), y, z, 1 - c)),
        st.go(feat.at[pl.ds(0, 272)], F.at[pl.ds(560, 272)], dev(xp, y, z, c)),
        st.go(feat.at[pl.ds(240, 272)], F.at[pl.ds(832, 272)], dev(xm, y, z, c)),
    ]
    start_zA(1)

    own_q.wait()
    for k in range(3):
        w = QT[k]
        QT[k] = jnp.concatenate(
            [w[:, (2 * b + a) * HEAD:(2 * b + a + 1) * HEAD] for a in range(2) for b in range(4)], axis=1
        )
    mine_q = AW.at[:, z, y, :, cols]
    swap_q = st.make(QT.at[:, :, cols], mine_q, dev(3 - x, y, z, c), pend=False)
    keep_q = pltpu.make_async_copy(QT.at[:, :, cols], mine_q, ls.at[4])

    @pl.when(hi == 0)
    def _():
        swap_q.start()
        keep_q.start()

    swap_o = st.go(out_in.at[:, cols], OW.at[lo, z, y, :, cols], dev(3 - x, y, z, c))

    acc[...] = jnp.zeros_like(acc)
    own_f.wait()
    own_w.wait()
    own_o.wait()

    def ready_features():
        for cp in halo:
            cp.wait_recv()
        sa = 2 * lax.div(xm, 2) + c
        sbk = 2 * lax.div(xp, 2) + c
        for cond, at in ((s == 0, 0), (s == 3, 528), (sa == 0, 544), (sbk == 3, 1104)):
            @pl.when(cond)
            def _(at=at):
                F[at:at + 16] = jnp.zeros((16, D), BF)

    def conv_tap(t):
        for cp in sb[t]:
            cp.wait_recv()

        def body(n, carry):
            at = al(n * 256, 256)
            out = nt(F[...], CW[t, pl.ds(at, 256), :])
            for j in range(2):
                acc[2 * n + j, 4 - t:4 - t + ROWS] += out[:, 128 * j:128 * j + 128]
            return carry

        lax.fori_loop(0, 3, body, 0)

    i0, k0 = (1 - c) * y + c * z, (1 - c) * z + c * y

    class Gather:
        def __init__(self, buf):
            self.buf = buf
            self.a2, self.b2 = {}, {}

        def ref(self, i, k, sub=None):
            zz, yy = (1 - c) * k + c * i, (1 - c) * i + c * k
            if sub is None:
                return self.buf.at[:, zz, yy, :, cols]
            return self.buf.at[:, zz, yy, :, pl.ds(al(c * HALF + 384 * sub, 128), 384)]

        def to(self, i, k):
            return dev(x, (1 - c) * i + c * k, (1 - c) * k + c * i, c)

        def second(self, j):
            i = m4(i0 + j)
            own = self.ref(i, k0)
            self.a2[j] = [same(own, self.to(i0, m4(k0 + d))) for d in (1, -1)]

        def second_pass(self, j):
            i = m4(i0 + j)
            self.a2[j][0].wait_recv()
            self.b2[j] = [same(self.ref(i, m4(k0 - 1), 0), self.to(i0, m4(k0 + 1)))]
            self.a2[j][1].wait_recv()
            self.b2[j].append(same(self.ref(i, m4(k0 + 1), 1), self.to(i0, m4(k0 - 1))))

        def p0(self):
            own = self.ref(i0, k0)
            self.a1 = [same(own, self.to(m4(i0 + d), k0)) for d in (1, -1)]
            self.second(0)

        def p1(self):
            self.a1[0].wait_recv()
            self.b1 = [same(self.ref(m4(i0 - 1), k0, 0), self.to(m4(i0 + 1), k0))]
            self.second(-1)
            self.a1[1].wait_recv()
            self.b1.append(same(self.ref(m4(i0 + 1), k0, 1), self.to(m4(i0 - 1), k0)))
            self.second(1)

        def p2(self):
            self.second_pass(0)
            for cp in self.b1:
                cp.wait_recv()
            self.second(2)

        def p3(self):
            self.second_pass(-1)
            self.second_pass(1)

        def p4(self):
            self.second_pass(2)

        def p5(self):
            for j in (0, -1, 1, 2):
                for cp in self.b2[j]:
                    cp.wait_recv()

    gq, go = Gather(AW), Gather(OW)

    order = [0, 1, 2, 3, 4]
    for step in range(7):
        if step < 5:
            pass_zA(order[step])
            if step + 2 < 5:
                start_zA(order[step + 2])
        if step == 4:
            @pl.when(hi == 0)
            def _():
                keep_q.wait()

            @pl.when(hi == 1)
            def _():
                swap_q.wait_recv()
            gq.p0()
        if 1 <= step < 6:
            pass_zB(order[step - 1])
        if step == 5:
            gq.p1()
        if step >= 2:
            if step == 2:
                ready_features()
            pass_yC(order[step - 2])
            conv_tap(order[step - 2])

    gq.p2()

    bias = vec[lo]
    wo = 2 * z + (1 - lo)

    def tokens(at, window):
        species = vec[2 * (2 + window) + lo]
        cut = []
        for j in range(6):
            lanes = slice(128 * j, 128 * j + 128)
            even = jax.nn.gelu(acc[j, pl.ds(at, 128, stride=2), :] + bias[:, lanes])
            odd = jax.nn.gelu(acc[j, pl.ds(at + 1, 128, stride=2), :] + bias[:, lanes])
            cut.append((jnp.maximum(even, odd) + species[:, lanes]).astype(BF))
        return jnp.concatenate(cut, axis=1)

    TA[0:128] = tokens(562, wo)
    TA[128:256] = tokens(850, wo)
    a0 = (2 * lax.div(xm, 2) + c) * 256
    b0 = (2 * lax.div(xp, 2) + c) * 256 + 128
    ta, tb = TH.at[lo, pl.ds(al(a0, 128), 128)], TH.at[lo, pl.ds(al(b0, 128), 128)]
    cross = []
    for xx in (xp, xm):
        cross += [
            st.go(TA.at[pl.ds(0, 128)], ta, dev(xx, y, z, c)),
            st.go(TA.at[pl.ds(128, 128)], tb, dev(xx, y, z, c)),
        ]
    TH[lo, pl.ds(al(s * 256, 256), 128)] = tokens(18, p)
    TH[lo, pl.ds(al(s * 256 + 128, 128), 128)] = tokens(274, p)
    s2 = 2 * (1 - hi) + c
    blk = pl.ds(al(s * 256, 256), 256)
    blk2 = pl.ds(al(s2 * 256, 256), 256)
    far = same(TH.at[lo, blk], dev(x2, y, z, c))
    near = [same(TH.at[lo, blk], sib)]

    gq.p3()
    for cp in cross:
        cp.wait_recv()
    near.append(same(TH.at[1 - lo, blk], sib))
    far.wait_recv()
    near.append(same(TH.at[lo, blk2], sib))
    near.append(same(TH.at[1 - lo, blk2], sib))
    gq.p4()
    gq.p5()
    other = pl.ds(al(2 * (1 - c), 2), 2)
    sq = same(AW.at[:, other, :, :, cols], sib)
    swap_o.wait_recv()
    go.p0()

    def norm(block):
        at = pl.ds(al(block * 256, 256), 256)
        h0 = TH[0, at].astype(F32)
        h1 = TH[1, at].astype(F32)
        ms = (jnp.sum(h0 * h0, axis=1, keepdims=True) + jnp.sum(h1 * h1, axis=1, keepdims=True)) / D
        r = lax.rsqrt(ms + 1e-05)
        NM[at, 0:HALF] = (h0 * r * vec[2]).astype(BF)
        NM[at, HALF:D] = (h1 * r * vec[3]).astype(BF)

    norm(s)
    norm(s2)
    hs = [TH[a, blk] for a in range(2)]
    TOK[...] = jnp.concatenate([hs[a][:, b * HEAD:(b + 1) * HEAD] for b in range(4) for a in range(2)], axis=1)
    go.p1()
    for cp in near:
        cp.wait_recv()
    norm(2 * hi + 1 - c)
    norm(2 * (1 - hi) + 1 - c)
    go.p2()
    sq.wait_recv()

    for part in range(3):
        w = AW[part, pl.ds(al(2 * c, 2), 2)].reshape(2 * HEAD, D)
        res = nt(NM[...], w).astype(BF)
        for h in range(2):
            QH[part, h] = res[:, h * HEAD:(h + 1) * HEAD]
    go.p3()

    scale = 1.0 / math.sqrt(HEAD)
    lop = lax.rem(lo + hi, 2)
    my_cols = pl.ds(al((2 * lop + c) * 384, 128), 384)
    back = []
    dests = [(1 - hi, c, x2, c), (1 - hi, 1 - c, x2, 1 - c), (hi, 1 - c, x, 1 - c), (hi, c, None, None)]
    for d, (dhi, dc, dx, dcc) in enumerate(dests):
        at = pl.ds(al((2 * dhi + dc) * 256, 256), 256)
        for h in range(2):
            sc = nt(QH[0, h, at], QH[1, h]) * scale
            e = jnp.exp(sc - jnp.max(sc, axis=1, keepdims=True))
            inv = 1.0 / jnp.sum(e, axis=1, keepdims=True)
            AO[d, h] = (nn(e.astype(BF), QH[2, h]) * inv).astype(BF)
        both = jnp.concatenate([AO[d, 0], AO[d, 1]], axis=1)
        if dx is None:
            AT[:, my_cols] = both
        else:
            NM[d * 256:(d + 1) * 256, 0:384] = both
            back.append(st.go(NM.at[pl.ds(d * 256, 256), pl.ds(0, 384)], AT.at[:, my_cols], dev(dx, y, z, dcc)))
        if d == 1:
            go.p4()
            go.p5()
            so = same(OW.at[:, :, :, :, cols], sib)

    so.wait_recv()
    for cp in back:
        cp.wait_recv()

    def out_body(n, carry):
        at = pl.ds(al(n * 256, 256), 256)
        mixed = nn(AT[...], OW[:, :, :, :, at].reshape(D, 256))
        seq_out[:, at] = (TOK[:, at].astype(F32) + mixed).astype(BF)
        return carry

    lax.fori_loop(0, 6, out_body, 0)

    rows = jnp.sum(seq_out[...].astype(F32).reshape(16, POOL, D), axis=1) * (1.0 / POOL)
    unit = (rows * lax.rsqrt(jnp.mean(rows * rows, axis=1, keepdims=True) + 1e-05)).astype(BF)
    left_out[...] = nn(unit, lw[...]).astype(BF)
    right_out[...] = nn(unit, rw[...]).astype(BF).astype(F32)

    for cp in st.all:
        cp.wait_send()

    @pl.when(hi == 0)
    def _():
        swap_q.wait_send()


def pair_kernel(left, right, mix, out, L, R, ssl, rsl, ssr, rsr):
    s, p, y, hi, c, z, lo, x = coords()
    barrier = pltpu.get_barrier_semaphore()
    inside = lax.div(p, 2) == s
    for d in range(1, 8):
        pl.semaphore_signal(barrier, inc=1, device_id=(s, lax.rem(p + d, 8), y), device_id_type=MESH)
    for w in range(8):
        @pl.when(jnp.logical_not(jnp.logical_and(inside, p == w)))
        def _(w=w):
            pl.semaphore_signal(barrier, inc=1, device_id=(lax.div(p, 2), w, y), device_id_type=MESH)
    pl.semaphore_wait(barrier, 15 - inside.astype(jnp.int32))

    lefts = []
    for d in range(1, 8):
        cp = pltpu.make_async_remote_copy(
            src_ref=left, dst_ref=L.at[p], send_sem=ssl.at[d], recv_sem=rsl.at[d],
            device_id=(s, lax.rem(p + d, 8), y), device_id_type=MESH,
        )
        cp.start()
        lefts.append(cp)
    L[p] = left[...]

    def right_copy(q, half):
        return pltpu.make_async_remote_copy(
            src_ref=right.at[pl.ds(8 * half, 8)], dst_ref=R.at[p], send_sem=ssr.at[2 * q + half],
            recv_sem=rsr.at[p], device_id=(q, 2 * s + half, y), device_id_type=MESH,
        )

    for q in range(4):
        for half in range(2):
            me = jnp.logical_and(p == 2 * s + half, q == s)

            @pl.when(jnp.logical_not(me))
            def _(q=q, half=half):
                right_copy(q, half).start()

            @pl.when(me)
            def _(half=half):
                R[p] = right[8 * half:8 * half + 8, :]

    for cp in lefts:
        cp.wait_recv()
    for w in range(8):
        @pl.when(jnp.logical_not(jnp.logical_and(inside, p == w)))
        def _(w=w):
            pltpu.make_async_remote_copy(
                src_ref=right.at[pl.ds(0, 8)], dst_ref=R.at[w], send_sem=ssr.at[0],
                recv_sem=rsr.at[w], device_id=(s, p, y), device_id_type=MESH,
            ).wait_recv()

    outer = L[...].astype(F32)[:, :, None, :] * R[...][:, None, :, :]
    out[...] = nn(outer.reshape(1024, 128).astype(BF), mix[...]).astype(BF)
    for cp in lefts:
        cp.wait_send()
    for q in range(4):
        for half in range(2):
            @pl.when(jnp.logical_not(jnp.logical_and(p == 2 * s + half, q == s)))
            def _(q=q, half=half):
                right_copy(q, half).wait_send()


def local(
    features, conv_weight, conv_bias, species_table, species_id, norm_gain,
    qkv_weight, out_weight, left_weight, right_weight, mix_weight,
):
    species_rows = jnp.where(species_id[0][:, None] == 0, species_table[0][None, :], species_table[1][None, :])
    vec = jnp.concatenate([conv_bias[None], norm_gain[None], species_rows], axis=0)
    vec = vec.reshape(10, 4, 2, HEAD).transpose(0, 2, 1, 3).reshape(20, 1, HALF)
    any_ = pl.BlockSpec(memory_space=pl.ANY)
    vm = pl.BlockSpec(memory_space=pltpu.VMEM)
    seq_out, left, right = pl.pallas_call(
        main_kernel,
        out_shape=(
            jax.ShapeDtypeStruct((256, D), BF),
            jax.ShapeDtypeStruct((16, 128), BF),
            jax.ShapeDtypeStruct((16, 128), F32),
        ),
        in_specs=[any_, any_, any_, any_, vm, vm, vm],
        out_specs=(vm, vm, vm),
        scratch_shapes=[
            pltpu.VMEM((ROWS, D), BF),
            pltpu.VMEM((5, HALF, D), BF),
            pltpu.VMEM((6, ROWS + 8, 128), F32),
            pltpu.VMEM((3, 48, D), BF),
            pltpu.VMEM((3, 4, 4, 48, D), BF),
            pltpu.VMEM((2, 4, 4, 48, D), BF),
            pltpu.VMEM((2, 1024, HALF), BF),
            pltpu.VMEM((256, HALF), BF),
            pltpu.VMEM((256, D), BF),
            pltpu.VMEM((1024, D), BF),
            pltpu.VMEM((3, 2, 1024, HEAD), BF),
            pltpu.VMEM((4, 2, 256, HEAD), BF),
            pltpu.VMEM((256, D), BF),
            pltpu.SemaphoreType.DMA((N_SITES,)),
            pltpu.SemaphoreType.DMA((N_SITES,)),
            pltpu.SemaphoreType.DMA((5,)),
        ],
        compiler_params=pltpu.CompilerParams(
            collective_id=0, has_side_effects=True, vmem_limit_bytes=62 * 2**20
        ),
        name="window",
    )(features.reshape(512, D), conv_weight, qkv_weight, out_weight, vec, left_weight, right_weight)
    pair_map = pl.pallas_call(
        pair_kernel,
        out_shape=jax.ShapeDtypeStruct((1024, 128), BF),
        in_specs=[vm, vm, vm],
        out_specs=vm,
        scratch_shapes=[
            pltpu.VMEM((8, 16, 128), BF),
            pltpu.VMEM((8, 8, 128), F32),
            pltpu.SemaphoreType.DMA((8,)),
            pltpu.SemaphoreType.DMA((8,)),
            pltpu.SemaphoreType.DMA((8,)),
            pltpu.SemaphoreType.DMA((8,)),
        ],
        compiler_params=pltpu.CompilerParams(collective_id=1, has_side_effects=True),
        name="pairs",
    )(left, right, mix_weight)
    return seq_out[None, None], pair_map.reshape(1, 8, 16, 8, 128)


def solution(mesh):
    return jax.shard_map(
        local,
        mesh=mesh,
        in_specs=(
            P("dp", "pair", "seq", None),
            P(None, "pair", None),
            P(),
            P(),
            P("dp", None),
            P(),
            P(None, ("pair", "dp"), None),
            P(("pair", "dp"), None),
            P(),
            P(),
            P(),
        ),
        out_specs=(P("dp", "pair", "seq", None), P("dp", None, "seq", "pair", None)),
        check_vma=False,
    )
```

time: 736 us -> 138 us (0.19)
  waiting for transfers between devices: 527 us -> 0 us
  Pallas kernels: 0 us -> 129 us
  blocking collectives: 76.6 us -> 0 us
  matrix products: 69.7 us -> 0 us
  local copies, waits for them, and re-layouts: 23 us -> 7.05 us
  between operations: 14 us -> 0.67 us
  starting transfers between devices: 11.6 us -> 0 us
    all_gather x4 -> x0, waiting for transfers between devices: 522 us -> none  [the longest x1 248 us: local(): piece = lax.all_gather(haloed, 'pair', axis=1, tiled=True)]
    pallas_call x0 -> x2, Pallas kernels: none -> 129 us  [the longest x1 121 us: local(): pl.pallas_call(main_kernel, out_shape=(jax.ShapeDtypeStruct((256, D), BF)...]
    dot_general x13 -> x0, matrix products: 61.3 us -> none  [the longest x5 36.7 us: local(): jnp.einsum('gnrd,ed->gnre', piece[:, :, shift:shift + length], conv_weigh...]
    all_gather x2 -> x0, blocking collectives: 46.9 us -> none  [the longest x1 24.6 us: local(): column_all = lax.all_gather(right, 'seq', axis=2, tiled=True)]
    all_to_all x1 -> x0, blocking collectives: 29.8 us -> none  [local(): lax.all_to_all(sliced, 'pair', split_axis=1, concat_axis=3, tiled=True)]
    slice x4 -> x1, local copies, waits for them, and re-layouts: 13.4 us -> 0.82 us  [local(): species_table[0][None, :]]
    sub x1 -> x0, matrix products: 8.41 us -> none  [attend_heads(): weights = jax.nn.softmax(scores, axis=-1).astype(jnp.bfloat16)]
    ppermute x2 -> x0, starting transfers between devices: 8.09 us -> none  [the longest x1 6.17 us: extended(): lax.ppermute(lax.slice_in_dim(block, block.shape[dim] - width, None, axis...]
  transfers between devices with their start and end apart: 7 -> 0, of which waited for: 5 -> 0; matrix products, arithmetic and copies ran while one was open for 11% -> 0% of each run, Pallas kernels for 0% -> 0%
where the time goes in v1:
time: 138 us
  Pallas kernels  129 us (93%)
  local copies, waits for them, and re-layouts  7.05 us (5%)
    pallas_call x1, Pallas kernels, local(): pl.pallas_call(main_kernel, out_shape=(jax.ShapeDtypeStruct((256, D), BF)...  121 us
    pallas_call x1, Pallas kernels, local(): pl.pallas_call(pair_kernel, out_shape=jax.ShapeDtypeStruct((1024, 128), B...  8.24 us
    unnamed x2, local copies, waits for them, and re-layouts  3.73 us

profile of v1, /device:TPU:1, one launch (start us, length us, event | category | flops | bytes accessed | tf_op | source)
XLA Modules:
  0.0 137.7 jit_solution(7512740882251351252)
XLA Ops:
  0.6 0.7 compare_bitcast_fusion
  1.3 0.8 concatenate.8
  2.1 0.8 concatenate.9
  2.9 0.8 slice_reduce_fusion.1
  3.7 0.1 broadcast_in_dim.34
  3.8 0.1 broadcast_in_dim.36
  3.8 0.1 broadcast_select_fusion
  4.0 0.8 reshape.44.vec
  4.7 120.9 %window.1 = (bf16[256,1536]{1,0:T(8,128)(2,1)}, bf16[16,128]{1,0:T(8,128)(2,1)}, f32[16,128]{1,0:T(8,128)}) custom-call(bf16[512,1536]{1,0:T(8,128)(2,1)} %bitcast.7, bf16[5,192,1536]{2,1,0:T(8,128)(2,1)} %cw_in.1, bf16[3,48,1536]{2,1,0:T(8,128)(2,1)} %qkv_in.1, bf16[48,1536]{1,0:T(8,128)(2,1)} %out_in.1, f32[20,1,768]{2,1,0:T(1,128)} %reshape.44.vec, ...), custom_call_target="tpu_custom_call" | custom-call | tf_op jit(solution)/shard_map/window/pallas_call | solution.py:484
  125.7 8.2 %pairs.1 = bf16[1024,128]{1,0:T(8,128)(2,1)} custom-call(bf16[16,128]{1,0:T(8,128)(2,1)} %get-tuple-element.6.left, f32[16,128]{1,0:T(8,128)} %get-tuple-element.7.right, bf16[128,128]{1,0:T(8,128)(2,1)} %mix.1), custom_call_target="tpu_custom_call" | custom-call | tf_op jit(solution)/shard_map/pairs/pallas_call | solution.py:516
  133.9 2.1 %copy.21 = bf16[1,1,256,1536]{3,2,1,0:T(8,128)(2,1)} copy(bf16[1,1,256,1536]{3,2,1,0:T(8,128)(2,1)} %bitcast.9) | data formatting | bytes 1572864
  136.0 1.7 %copy.22 = bf16[1,8,16,8,128]{4,3,2,1,0:T(8,128)(2,1)} copy(bf16[1,8,16,8,128]{4,3,2,1,0:T(8,128)(2,1)} %bitcast.8) | data formatting | bytes 524288
  (5 shorter events, 0.0 us)

commit v2 on v1

--- a/solution.py
+++ b/solution.py
@@ -66,13 +66,21 @@
         return cp
 
 
-N_SITES = 128
+N_SITES = 160
+CHUNKS = [(n, lo, hi) for n in range(3) for lo, hi in ((0, 3), (3, 5))]
+
+
+def by_window(v):
+    return jnp.concatenate(
+        [v[:, at:at + 64] for a in range(2) for n in range(3) for at in [(2 * b + a) * HEAD + n * 64 for b in range(4)]],
+        axis=1,
+    )
 
 
 def main_kernel(
-    feat, cw_in, qkv_in, out_in, vec, lw, rw,
+    feat, cw_in, qkv_in, out_in, bias_in, gain_in, table_in, id_in, lw, rw,
     seq_out, left_out, right_out,
-    F, CW, acc, QT, AW, OW, TH, TA, TOK, NM, QH, AO, AT,
+    F, CW, acc, QT, AW, OW, TH, TA, TOK, NM, QH, AO, AT, VEC,
     ss, rs, ls,
 ):
     s, p, y, hi, c, z, lo, x = coords()
@@ -101,45 +109,49 @@
     own_q = local(qkv_in, QT)
     own_f = local(feat, F.at[pl.ds(16, 512)])
     own_o = local(out_in.at[:, cols], OW.at[lo, z, y, :, cols])
-    own_w = local(cw_in, CW.at[:, pl.ds(al(z * HEAD, 16), HEAD)])
+    own_w = [local(cw_in.at[:, pl.ds(64 * n, 64)], CW.at[n, :, pl.ds(al(z * 64, 16), 64)]) for n in range(3)]
     pl.semaphore_wait(barrier, len(peers))
 
     sgn = 1 - 2 * lax.rem(y + c, 2)
     zd, zs, zo = m4(z + sgn), m4(z - sgn), m4(z + 2)
     g = lax.rem(y + c, 2)
-    r0 = c * 96
     to_z = dev(x, y, zd, c)
 
-    def rows_of(slot, off, n):
-        return pl.ds(al(slot * HEAD + r0 + off, 16), n)
+    def part(k, slot, off, rows):
+        n, t0, t1 = CHUNKS[k]
+        return CW.at[n, pl.ds(t0, t1 - t0), pl.ds(al(slot * 64 + c * 32 + off, 16), rows)]
 
     zA, zB, yA, yC, sb = {}, {}, {}, {}, {}
-
-    def start_zA(t):
-        zA[t] = st.go(cw_in.at[t, pl.ds(al(r0, 16), 96)], CW.at[t, rows_of(z, 0, 96)], to_z)
 
     def same(ref, device):
         return st.go(ref, ref, device)
 
-    def pass_zA(t):
-        zA[t].wait_recv()
-        zB[t] = same(CW.at[t, rows_of(zs, 48 * g, 48)], to_z)
-        yA[t] = [
-            same(CW.at[t, rows_of(zs, 0, 48)], dev(x, m4(y + 1), z, c)),
-            same(CW.at[t, rows_of(zs, 48, 48)], dev(x, m4(y - 1), z, c)),
+    def start_zA(k):
+        if k < len(CHUNKS):
+            n, t0, t1 = CHUNKS[k]
+            src = cw_in.at[pl.ds(t0, t1 - t0), pl.ds(al(n * 64 + c * 32, 16), 32)]
+            zA[k] = st.go(src, part(k, z, 0, 32), to_z)
+
+    def pass_zA(k):
+        zA[k].wait_recv()
+        zB[k] = same(part(k, zs, 16 * g, 16), to_z)
+        yA[k] = [
+            same(part(k, zs, 0, 16), dev(x, m4(y + 1), z, c)),
+            same(part(k, zs, 16, 16), dev(x, m4(y - 1), z, c)),
         ]
-        sb[t] = [same(CW.at[t, rows_of(zs, 0, 96)], sib)]
-
-    def pass_zB(t):
-        zB[t].wait_recv()
-        yC[t] = same(CW.at[t, rows_of(zo, 48 * g, 48)], dev(x, m4(y + 1 - 2 * c), z, c))
-        for cp in yA[t]:
+        sb[k] = [same(part(k, zs, 0, 32), sib)]
+        start_zA(k + 3)
+
+    def pass_zB(k):
+        zB[k].wait_recv()
+        yC[k] = same(part(k, zo, 16 * g, 16), dev(x, m4(y + 1 - 2 * c), z, c))
+        for cp in yA[k]:
             cp.wait_recv()
-        sb[t].append(same(CW.at[t, rows_of(zd, 0, 96)], sib))
-
-    def pass_yC(t):
-        yC[t].wait_recv()
-        sb[t].append(same(CW.at[t, rows_of(zo, 0, 96)], sib))
+        sb[k].append(same(part(k, zd, 0, 32), sib))
+
+    def pass_yC(k):
+        yC[k].wait_recv()
+        sb[k].append(same(part(k, zo, 0, 32), sib))
 
     start_zA(0)
 
@@ -155,28 +167,24 @@
         st.go(feat.at[pl.ds(240, 272)], F.at[pl.ds(832, 272)], dev(xm, y, z, c)),
     ]
     start_zA(1)
-
+    start_zA(2)
+
+    VEC[0:1] = by_window(bias_in[...])
+    VEC[1:2] = by_window(gain_in[...])
+    VEC[2:4] = by_window(table_in[...])
     own_q.wait()
     for k in range(3):
-        w = QT[k]
-        QT[k] = jnp.concatenate(
-            [w[:, (2 * b + a) * HEAD:(2 * b + a + 1) * HEAD] for a in range(2) for b in range(4)], axis=1
-        )
+        QT[k] = by_window(QT[k])
     mine_q = AW.at[:, z, y, :, cols]
     swap_q = st.make(QT.at[:, :, cols], mine_q, dev(3 - x, y, z, c), pend=False)
-    keep_q = pltpu.make_async_copy(QT.at[:, :, cols], mine_q, ls.at[4])
-
-    @pl.when(hi == 0)
-    def _():
-        swap_q.start()
-        keep_q.start()
-
-    swap_o = st.go(out_in.at[:, cols], OW.at[lo, z, y, :, cols], dev(3 - x, y, z, c))
+    keep_q = pltpu.make_async_copy(QT.at[:, :, cols], mine_q, ls.at[6])
+    swap_o = st.make(out_in.at[:, cols], OW.at[lo, z, y, :, cols], dev(3 - x, y, z, c))
 
     acc[...] = jnp.zeros_like(acc)
     own_f.wait()
-    own_w.wait()
     own_o.wait()
+    for cp in own_w:
+        cp.wait()
 
     def ready_features():
         for cp in halo:
@@ -188,18 +196,31 @@
             def _(at=at):
                 F[at:at + 16] = jnp.zeros((16, D), BF)
 
-    def conv_tap(t):
-        for cp in sb[t]:
-            cp.wait_recv()
-
-        def body(n, carry):
-            at = al(n * 256, 256)
-            out = nt(F[...], CW[t, pl.ds(at, 256), :])
-            for j in range(2):
-                acc[2 * n + j, 4 - t:4 - t + ROWS] += out[:, 128 * j:128 * j + 128]
-            return carry
-
-        lax.fori_loop(0, 3, body, 0)
+    def start_swap():
+        @pl.when(hi == 0)
+        def _():
+            swap_q.start()
+            keep_q.start()
+        swap_o.start()
+
+    def wait_swap():
+        @pl.when(hi == 0)
+        def _():
+            keep_q.wait()
+
+        @pl.when(hi == 1)
+        def _():
+            swap_q.wait_recv()
+
+    def conv_ready(n):
+        for k in (2 * n, 2 * n + 1):
+            for cp in sb[k]:
+                cp.wait_recv()
+
+    def conv_tap(n, t):
+        out = nt(F[...], CW[n, t])
+        for j in range(2):
+            acc[2 * n + j, 4 - t:4 - t + ROWS] += out[:, 128 * j:128 * j + 128]
 
     i0, k0 = (1 - c) * y + c * z, (1 - c) * z + c * y
 
@@ -262,105 +283,144 @@
 
     gq, go = Gather(AW), Gather(OW)
 
-    order = [0, 1, 2, 3, 4]
-    for step in range(7):
-        if step < 5:
-            pass_zA(order[step])
-            if step + 2 < 5:
-                start_zA(order[step + 2])
-        if step == 4:
-            @pl.when(hi == 0)
-            def _():
-                keep_q.wait()
-
-            @pl.when(hi == 1)
-            def _():
-                swap_q.wait_recv()
-            gq.p0()
-        if 1 <= step < 6:
-            pass_zB(order[step - 1])
-        if step == 5:
-            gq.p1()
-        if step >= 2:
-            if step == 2:
-                ready_features()
-            pass_yC(order[step - 2])
-            conv_tap(order[step - 2])
-
-    gq.p2()
-
-    bias = vec[lo]
-    wo = 2 * z + (1 - lo)
-
-    def tokens(at, window):
-        species = vec[2 * (2 + window) + lo]
-        cut = []
-        for j in range(6):
-            lanes = slice(128 * j, 128 * j + 128)
-            even = jax.nn.gelu(acc[j, pl.ds(at, 128, stride=2), :] + bias[:, lanes])
-            odd = jax.nn.gelu(acc[j, pl.ds(at + 1, 128, stride=2), :] + bias[:, lanes])
-            cut.append((jnp.maximum(even, odd) + species[:, lanes]).astype(BF))
-        return jnp.concatenate(cut, axis=1)
-
-    TA[0:128] = tokens(562, wo)
-    TA[128:256] = tokens(850, wo)
-    a0 = (2 * lax.div(xm, 2) + c) * 256
-    b0 = (2 * lax.div(xp, 2) + c) * 256 + 128
-    ta, tb = TH.at[lo, pl.ds(al(a0, 128), 128)], TH.at[lo, pl.ds(al(b0, 128), 128)]
-    cross = []
-    for xx in (xp, xm):
-        cross += [
-            st.go(TA.at[pl.ds(0, 128)], ta, dev(xx, y, z, c)),
-            st.go(TA.at[pl.ds(128, 128)], tb, dev(xx, y, z, c)),
-        ]
-    TH[lo, pl.ds(al(s * 256, 256), 128)] = tokens(18, p)
-    TH[lo, pl.ds(al(s * 256 + 128, 128), 128)] = tokens(274, p)
     s2 = 2 * (1 - hi) + c
     blk = pl.ds(al(s * 256, 256), 256)
     blk2 = pl.ds(al(s2 * 256, 256), 256)
-    far = same(TH.at[lo, blk], dev(x2, y, z, c))
-    near = [same(TH.at[lo, blk], sib)]
-
+    a0 = (2 * lax.div(xm, 2) + c) * 256
+    b0 = (2 * lax.div(xp, 2) + c) * 256 + 128
+    ids = id_in[...]
+    lane = lax.broadcasted_iota(jnp.int32, (1, 8), 1)
+
+    def piece(row, n):
+        both = [VEC[row:row + 1, a * HALF + n * 256:a * HALF + n * 256 + 256] for a in range(2)]
+        return jnp.where(jnp.full((1, 256), lo, jnp.int32) == 0, both[0], both[1])
+
+    def tokens(at, window, n):
+        kind = jnp.sum(jnp.where(lane == window, ids, 0), axis=1, keepdims=True)
+        species = jnp.where(jnp.broadcast_to(kind, (1, 256)) == 0, piece(2, n), piece(3, n))
+        bias = piece(0, n)
+        cut = []
+        for j in range(2):
+            lanes = slice(128 * j, 128 * j + 128)
+            even = jax.nn.gelu(acc[2 * n + j, pl.ds(at, 128, stride=2), :] + bias[:, lanes])
+            odd = jax.nn.gelu(acc[2 * n + j, pl.ds(at + 1, 128, stride=2), :] + bias[:, lanes])
+            cut.append((jnp.maximum(even, odd) + species[:, lanes]).astype(BF))
+        return jnp.concatenate(cut, axis=1)
+
+    cross, far, near = {}, {}, {}
+
+    def send_tokens(n):
+        wo = 2 * z + (1 - lo)
+        TA[n, 0:128] = tokens(562, wo, n)
+        TA[n, 128:256] = tokens(850, wo, n)
+        ta, tb = TH.at[lo, n, pl.ds(al(a0, 128), 128)], TH.at[lo, n, pl.ds(al(b0, 128), 128)]
+        cross[n] = []
+        for xx in (xp, xm):
+            cross[n] += [
+                st.go(TA.at[n, pl.ds(0, 128)], ta, dev(xx, y, z, c)),
+                st.go(TA.at[n, pl.ds(128, 128)], tb, dev(xx, y, z, c)),
+            ]
+        TH[lo, n, pl.ds(al(s * 256, 256), 128)] = tokens(18, p, n)
+        TH[lo, n, pl.ds(al(s * 256 + 128, 128), 128)] = tokens(274, p, n)
+        far[n] = same(TH.at[lo, n, blk], dev(x2, y, z, c))
+        near[n] = [same(TH.at[lo, n, blk], sib)]
+
+    def pass_tokens(n):
+        for cp in cross[n]:
+            cp.wait_recv()
+        near[n].append(same(TH.at[1 - lo, n, blk], sib))
+        near[n].append(same(TH.at[1 - lo, n, blk2], sib))
+        far[n].wait_recv()
+        near[n].append(same(TH.at[lo, n, blk2], sib))
+
+    def norm(block):
+        at = pl.ds(al(block * 256, 256), 256)
+        ms = 0.0
+        for a in range(2):
+            for n in range(3):
+                h = TH[a, n, at].astype(F32)
+                ms = ms + jnp.sum(h * h, axis=1, keepdims=True)
+        r = lax.rsqrt(ms / D + 1e-05)
+        for a in range(2):
+            for n in range(3):
+                lanes = slice(a * HALF + n * 256, a * HALF + n * 256 + 256)
+                NM[at, lanes] = (TH[a, n, at].astype(F32) * r * VEC[1:2, lanes]).astype(BF)
+
+    pass_zA(0)
+    pass_zA(1)
+    pass_zB(0)
+    pass_zA(2)
+    pass_zB(1)
+    pass_yC(0)
+    pass_zA(3)
+    pass_zB(2)
+    pass_yC(1)
+    ready_features()
+    start_swap()
+    conv_ready(0)
+    conv_tap(0, 0)
+    conv_tap(0, 1)
+    pass_zA(4)
+    pass_zB(3)
+    pass_yC(2)
+    conv_tap(0, 2)
+    conv_tap(0, 3)
+    conv_tap(0, 4)
+    pass_zA(5)
+    pass_zB(4)
+    pass_yC(3)
+    send_tokens(0)
+    pass_zB(5)
+    pass_yC(4)
+    wait_swap()
+    gq.p0()
+    conv_ready(1)
+    conv_tap(1, 0)
+    conv_tap(1, 1)
+    pass_yC(5)
+    conv_tap(1, 2)
+    conv_tap(1, 3)
+    gq.p1()
+    conv_tap(1, 4)
+    send_tokens(1)
+    conv_ready(2)
+    conv_tap(2, 0)
+    conv_tap(2, 1)
+    gq.p2()
+    conv_tap(2, 2)
+    conv_tap(2, 3)
+    pass_tokens(0)
+    conv_tap(2, 4)
+    send_tokens(2)
     gq.p3()
-    for cp in cross:
-        cp.wait_recv()
-    near.append(same(TH.at[1 - lo, blk], sib))
-    far.wait_recv()
-    near.append(same(TH.at[lo, blk2], sib))
-    near.append(same(TH.at[1 - lo, blk2], sib))
+    pass_tokens(1)
     gq.p4()
+    swap_o.wait_recv()
+    go.p0()
+    pass_tokens(2)
+    norm(s)
+    norm(s2)
+    hs = {(a, n): TH[a, n, blk] for a in range(2) for n in range(3)}
+    TOK[...] = jnp.concatenate(
+        [hs[a, n][:, b * 64:(b + 1) * 64] for b in range(4) for a in range(2) for n in range(3)], axis=1
+    )
     gq.p5()
     other = pl.ds(al(2 * (1 - c), 2), 2)
     sq = same(AW.at[:, other, :, :, cols], sib)
-    swap_o.wait_recv()
-    go.p0()
-
-    def norm(block):
-        at = pl.ds(al(block * 256, 256), 256)
-        h0 = TH[0, at].astype(F32)
-        h1 = TH[1, at].astype(F32)
-        ms = (jnp.sum(h0 * h0, axis=1, keepdims=True) + jnp.sum(h1 * h1, axis=1, keepdims=True)) / D
-        r = lax.rsqrt(ms + 1e-05)
-        NM[at, 0:HALF] = (h0 * r * vec[2]).astype(BF)
-        NM[at, HALF:D] = (h1 * r * vec[3]).astype(BF)
-
-    norm(s)
-    norm(s2)
-    hs = [TH[a, blk] for a in range(2)]
-    TOK[...] = jnp.concatenate([hs[a][:, b * HEAD:(b + 1) * HEAD] for b in range(4) for a in range(2)], axis=1)
     go.p1()
-    for cp in near:
-        cp.wait_recv()
+    for n in range(3):
+        for cp in near[n]:
+            cp.wait_recv()
     norm(2 * hi + 1 - c)
     norm(2 * (1 - hi) + 1 - c)
     go.p2()
     sq.wait_recv()
 
-    for part in range(3):
-        w = AW[part, pl.ds(al(2 * c, 2), 2)].reshape(2 * HEAD, D)
+    for k in range(3):
+        w = AW[k, pl.ds(al(2 * c, 2), 2)].reshape(2 * HEAD, D)
         res = nt(NM[...], w).astype(BF)
         for h in range(2):
-            QH[part, h] = res[:, h * HEAD:(h + 1) * HEAD]
+            QH[k, h] = res[:, h * HEAD:(h + 1) * HEAD]
     go.p3()
 
     scale = 1.0 / math.sqrt(HEAD)
@@ -381,8 +441,9 @@
         else:
             NM[d * 256:(d + 1) * 256, 0:384] = both
             back.append(st.go(NM.at[pl.ds(d * 256, 256), pl.ds(0, 384)], AT.at[:, my_cols], dev(dx, y, z, dcc)))
+        if d == 0:
+            go.p4()
         if d == 1:
-            go.p4()
             go.p5()
             so = same(OW.at[:, :, :, :, cols], sib)
 
@@ -476,9 +537,6 @@
     features, conv_weight, conv_bias, species_table, species_id, norm_gain,
     qkv_weight, out_weight, left_weight, right_weight, mix_weight,
 ):
-    species_rows = jnp.where(species_id[0][:, None] == 0, species_table[0][None, :], species_table[1][None, :])
-    vec = jnp.concatenate([conv_bias[None], norm_gain[None], species_rows], axis=0)
-    vec = vec.reshape(10, 4, 2, HEAD).transpose(0, 2, 1, 3).reshape(20, 1, HALF)
     any_ = pl.BlockSpec(memory_space=pl.ANY)
     vm = pl.BlockSpec(memory_space=pltpu.VMEM)
     seq_out, left, right = pl.pallas_call(
@@ -488,31 +546,35 @@
             jax.ShapeDtypeStruct((16, 128), BF),
             jax.ShapeDtypeStruct((16, 128), F32),
         ),
-        in_specs=[any_, any_, any_, any_, vm, vm, vm],
+        in_specs=[any_] * 4 + [vm] * 6,
         out_specs=(vm, vm, vm),
         scratch_shapes=[
             pltpu.VMEM((ROWS, D), BF),
-            pltpu.VMEM((5, HALF, D), BF),
+            pltpu.VMEM((3, 5, 256, D), BF),
             pltpu.VMEM((6, ROWS + 8, 128), F32),
             pltpu.VMEM((3, 48, D), BF),
             pltpu.VMEM((3, 4, 4, 48, D), BF),
             pltpu.VMEM((2, 4, 4, 48, D), BF),
-            pltpu.VMEM((2, 1024, HALF), BF),
-            pltpu.VMEM((256, HALF), BF),
+            pltpu.VMEM((2, 3, 1024, 256), BF),
+            pltpu.VMEM((3, 256, 256), BF),
             pltpu.VMEM((256, D), BF),
             pltpu.VMEM((1024, D), BF),
             pltpu.VMEM((3, 2, 1024, HEAD), BF),
             pltpu.VMEM((4, 2, 256, HEAD), BF),
             pltpu.VMEM((256, D), BF),
+            pltpu.VMEM((4, D), F32),
             pltpu.SemaphoreType.DMA((N_SITES,)),
             pltpu.SemaphoreType.DMA((N_SITES,)),
-            pltpu.SemaphoreType.DMA((5,)),
+            pltpu.SemaphoreType.DMA((7,)),
         ],
         compiler_params=pltpu.CompilerParams(
             collective_id=0, has_side_effects=True, vmem_limit_bytes=62 * 2**20
         ),
         name="window",
-    )(features.reshape(512, D), conv_weight, qkv_weight, out_weight, vec, left_weight, right_weight)
+    )(
+        features.reshape(512, D), conv_weight, qkv_weight, out_weight, conv_bias[None], norm_gain[None],
+        species_table, species_id, left_weight, right_weight,
+    )
     pair_map = pl.pallas_call(
         pair_kernel,
         out_shape=jax.ShapeDtypeStruct((1024, 128), BF),

time: 138 us -> 114 us (0.83)
  Pallas kernels: 129 us -> 107 us
    pallas_call x1, Pallas kernels: 121 us -> 98.8 us  [local(): pl.pallas_call(main_kernel, out_shape=(jax.ShapeDtypeStruct((256, D), BF)...]
    broadcast_in_dim x4 -> x2, local copies, waits for them, and re-layouts: 0.17 us -> 2.59 us  [the longest x1 1.3 us: local(): conv_bias[None]]
    concatenate x4 -> x0, local copies, waits for them, and re-layouts: 1.56 us -> none  [local(): jnp.concatenate([conv_bias[None], norm_gain[None], species_rows], axis=0)]
where the time goes in v2:
time: 114 us
  Pallas kernels  107 us (94%)
  local copies, waits for them, and re-layouts  6.32 us (6%)
    pallas_call x1, Pallas kernels, local(): pl.pallas_call(main_kernel, out_shape=(jax.ShapeDtypeStruct((256, D), BF)...  98.8 us
    pallas_call x1, Pallas kernels, local(): pl.pallas_call(pair_kernel, out_shape=jax.ShapeDtypeStruct((1024, 128), B...  8.16 us
    unnamed x2, local copies, waits for them, and re-layouts  3.73 us

profile of v2, /device:TPU:1, one launch (start us, length us, event | category | flops | bytes accessed | tf_op | source)
XLA Modules:
  0.0 114.0 jit_solution(2880117512036437543)
XLA Ops:
  0.6 1.3 %broadcast_in_dim.9.bias_in = f32[1,1536]{1,0:T(1,128)} reshape(f32[1536]{0:T(1024)} %param.13) | data formatting | bytes 12288 | tf_op jit(solution)/shard_map/broadcast_in_dim | solution.py:575
  1.9 1.3 %broadcast_in_dim.10.gain_in = f32[1,1536]{1,0:T(1,128)} reshape(f32[1536]{0:T(1024)} %param.16) | data formatting | bytes 12288 | tf_op jit(solution)/shard_map/broadcast_in_dim | solution.py:575
  3.2 98.8 %window.1 = (bf16[256,1536]{1,0:T(8,128)(2,1)}, bf16[16,128]{1,0:T(8,128)(2,1)}, f32[16,128]{1,0:T(8,128)}) custom-call(bf16[512,1536]{1,0:T(8,128)(2,1)} %bitcast.3, bf16[5,192,1536]{2,1,0:T(8,128)(2,1)} %cw_in.1, bf16[3,48,1536]{2,1,0:T(8,128)(2,1)} %qkv_in.1, bf16[48,1536]{1,0:T(8,128)(2,1)} %out_in.1, f32[1,1536]{1,0:T(1,128)} %broadcast_in_dim.9.bias_in, ...), custom_call_target="tpu_custom_call" | custom-call | tf_op jit(solution)/shard_map/window/pallas_call | solution.py:542
  102.0 8.2 %pairs.1 = bf16[1024,128]{1,0:T(8,128)(2,1)} custom-call(bf16[16,128]{1,0:T(8,128)(2,1)} %get-tuple-element.6.left, f32[16,128]{1,0:T(8,128)} %get-tuple-element.7.right, bf16[128,128]{1,0:T(8,128)(2,1)} %mix.1), custom_call_target="tpu_custom_call" | custom-call | tf_op jit(solution)/shard_map/pairs/pallas_call | solution.py:578
  110.2 2.1 %copy.15 = bf16[1,1,256,1536]{3,2,1,0:T(8,128)(2,1)} copy(bf16[1,1,256,1536]{3,2,1,0:T(8,128)(2,1)} %bitcast.5) | data formatting | bytes 1572864
  112.3 1.7 %copy.16 = bf16[1,8,16,8,128]{4,3,2,1,0:T(8,128)(2,1)} copy(bf16[1,8,16,8,128]{4,3,2,1,0:T(8,128)(2,1)} %bitcast.4) | data formatting | bytes 524288

commit v3 on v2

v3 whole, which is shorter than its diff:
```python
import math

import jax
import jax.numpy as jnp
from jax import lax
from jax.experimental import pallas as pl
from jax.experimental.pallas import tpu as pltpu
from jax.sharding import PartitionSpec as P

D = 1536
HEAD = 192
POOL = 16
SPECIES = 2
MESH = pl.DeviceIdType.MESH
BF = jnp.bfloat16
F32 = jnp.float32
HALF = 768
ROWS = 1120


def coords():
    s, p, y = lax.axis_index("seq"), lax.axis_index("pair"), lax.axis_index("dp")
    hi, c = lax.div(s, 2), lax.rem(s, 2)
    z, lo = lax.div(p, 2), lax.rem(p, 2)
    return s, p, y, hi, c, z, lo, 2 * hi + lo


def dev(x, y, z, c):
    return (2 * lax.div(x, 2) + c, 2 * z + lax.rem(x, 2), y)


def m4(v):
    return lax.rem(v + 4, 4)


def nt(a, b):
    return lax.dot_general(a, b, (((1,), (1,)), ((), ())), preferred_element_type=F32)


def nn(a, b):
    return lax.dot_general(a, b, (((1,), (0,)), ((), ())), preferred_element_type=F32)


def al(v, n):
    return pl.multiple_of(v, n)


class Sites:
    def __init__(self, ss, rs):
        self.ss, self.rs, self.n, self.all = ss, rs, 0, []

    def make(self, src, dst, device, pend=True):
        k = self.n
        self.n += 1
        cp = pltpu.make_async_remote_copy(
            src_ref=src, dst_ref=dst, send_sem=self.ss.at[k], recv_sem=self.rs.at[k],
            device_id=device, device_id_type=MESH,
        )
        if pend:
            self.all.append(cp)
        return cp

    def go(self, src, dst, device):
        cp = self.make(src, dst, device)
        cp.start()
        return cp

    def either(self, first, ref_a, ref_b, device):
        a = self.make(ref_a, ref_a, device)
        self.n -= 1
        b = self.make(ref_b, ref_b, device, pend=False)
        pl.when(first)(a.start)
        pl.when(jnp.logical_not(first))(b.start)
        return a


N_SITES = 240
CHUNKS = [
    (0, 0, 2), (0, 2, 4), (0, 4, 5),
    (1, 0, 2), (1, 2, 4), (1, 4, 5),
    (2, 0, 1), (2, 1, 3), (2, 3, 5),
]
ORDER = [
    ("Z", 0), ("Z", 1), ("A", 0), ("Z", 2), ("A", 1), ("Z", 3), ("B", 0), ("Y", 0), ("A", 2), ("Z", 4),
    ("B", 1), ("Y", 1), ("C", 0), ("Y", 2), ("A", 3), ("Z", 5), ("B", 2), ("C", 1), ("A", 4), ("Z", 6),
    ("Y", 3), ("B", 3), ("C", 2), ("A", 5), ("Z", 7), ("B", 4), ("Y", 4), ("A", 6), ("Z", 8), ("C", 3),
    ("B", 5), ("Y", 5), ("F", 0), ("T", 0, 0), ("T", 0, 1), ("A", 7), ("B", 6), ("C", 4), ("C", 5), ("Y", 6),
    ("T", 0, 2), ("T", 0, 3), ("A", 8), ("g0",), ("T", 0, 4), ("B", 7), ("C", 6), ("Y", 7), ("S", 0),
    ("T", 1, 0), ("B", 8), ("Y", 8), ("T", 1, 1), ("T", 1, 2), ("T", 1, 3), ("T", 1, 4), ("g+",), ("g-",),
    ("gP", 0), ("S", 1), ("X", 0), ("W", 0), ("C", 7), ("T", 2, 0), ("C", 8), ("T", 2, 1), ("gP", -1),
    ("T", 2, 2), ("gb",), ("T", 2, 3), ("T", 2, 4), ("gP", 1), ("S", 2), ("X", 1), ("W", 1), ("gP", 2),
    ("o0",), ("X", 2), ("W", 2), ("gQ",), ("N", 0), ("o+",), ("o-",), ("oP", 0), ("N", 1), ("V", 0), ("V", 1),
    ("ob",), ("oP", -1), ("D", 0), ("oP", 1), ("D", 1), ("oQ", 0), ("D", 2), ("oP", 2), ("D", 3), ("oQ", -1),
    ("oQ", 1), ("oQ", 2), ("O", 0), ("O", 1),
]


def by_window(v):
    return jnp.concatenate(
        [v[:, at:at + 64] for a in range(2) for n in range(3) for at in [(2 * b + a) * HEAD + n * 64 for b in range(4)]],
        axis=1,
    )


def main_kernel(
    feat, cw_in, qkv_in, out_in, bias_in, gain_in, table_in, id_in, lw, rw, mix,
    seq_out, pair_out,
    F, CW, acc, QT, AW, OW, TH, TA, TOK, NM, QH, AO, AT, BO, MX, VEC, LW, RW, L, R,
    ss, rs, ls, ssr, rsr,
):
    s, p, y, hi, c, z, lo, x = coords()
    xp, xm, x2 = m4(x + 1), m4(x - 1), m4(x + 2)
    sib = dev(x, y, z, 1 - c)
    st = Sites(ss, rs)

    barrier = pltpu.get_barrier_semaphore()
    peers = [sib]
    for xx in (xp, xm, x2):
        peers += [dev(xx, y, z, c), dev(xx, y, z, 1 - c)]
    for d in (1, -1):
        peers += [dev(x, m4(y + d), z, c), dev(x, y, m4(z + d), c)]
    peers += [(s, lax.rem(p + d, 8), y) for d in range(1, 8)]
    for t in peers:
        pl.semaphore_signal(barrier, inc=1, device_id=t, device_id_type=MESH)
    inside = lax.div(p, 2) == s
    for w in range(8):
        @pl.when(jnp.logical_not(jnp.logical_and(inside, p == w)))
        def _(w=w):
            pl.semaphore_signal(barrier, inc=1, device_id=(lax.div(p, 2), w, y), device_id_type=MESH)

    lcopies = []

    def local(src, dst):
        cp = pltpu.make_async_copy(src, dst, ls.at[len(lcopies)])
        cp.start()
        lcopies.append(cp)
        return cp

    cols = pl.ds(al(c * HALF, 128), HALF)
    own_q = local(qkv_in, QT)
    own_f = local(feat, F.at[pl.ds(16, 512)])
    own_o = local(out_in.at[:, cols], OW.at[lo, z, y, :, cols])
    own_w = [local(cw_in.at[:, pl.ds(64 * n, 64)], CW.at[n, :, pl.ds(al(z * 64, 16), 64)]) for n in range(3)]

    VEC[0:1] = by_window(bias_in[...].reshape(1, D))
    VEC[1:2] = by_window(gain_in[...].reshape(1, D))
    VEC[2:4] = by_window(table_in[...])
    own_q.wait()
    for k in range(3):
        QT[k] = by_window(QT[k])
    pl.semaphore_wait(barrier, len(peers) + 8 - inside.astype(jnp.int32))

    def turn(k):
        g = lax.rem(y + c, 2)
        sgn = 1 - 2 * g
        return g, m4(z + sgn), m4(z - sgn), m4(z + 2)

    def to_z(k):
        return dev(x, y, turn(k)[1], c)

    def part(k, slot, off, rows):
        n, t0, t1 = CHUNKS[k]
        return CW.at[n, pl.ds(t0, t1 - t0), pl.ds(al(slot * 64 + c * 32 + off, 16), rows)]

    zA, zB, yA, yC, sb = {}, {}, {}, {}, {}

    def same(ref, device):
        return st.go(ref, ref, device)

    def start_zA(k):
        n, t0, t1 = CHUNKS[k]
        src = cw_in.at[pl.ds(t0, t1 - t0), pl.ds(al(n * 64 + c * 32, 16), 32)]
        zA[k] = st.go(src, part(k, z, 0, 32), to_z(k))

    def pass_zA(k):
        zA[k].wait_recv()
        g, zd, zs, zo = turn(k)
        zB[k] = same(part(k, zs, 16 * g, 16), to_z(k))
        yA[k] = [
            same(part(k, zs, 0, 16), dev(x, m4(y + 1), z, c)),
            same(part(k, zs, 16, 16), dev(x, m4(y - 1), z, c)),
        ]
        sb[k] = [same(part(k, zs, 0, 32), sib)]

    def pass_zB(k):
        zB[k].wait_recv()
        g, zd, zs, zo = turn(k)
        yC[k] = same(part(k, zo, 16 * g, 16), dev(x, m4(y + 1 - 2 * c), z, c))

    def pass_yA(k):
        for cp in yA[k]:
            cp.wait_recv()
        sb[k].append(same(part(k, turn(k)[1], 0, 32), sib))

    def pass_yC(k):
        yC[k].wait_recv()
        sb[k].append(same(part(k, m4(z + 2), 0, 32), sib))

    start_zA(0)

    mine_q = AW.at[:, z, y, :, cols]
    inner = jnp.logical_or(x == 1, x == 2).astype(jnp.int32)
    third = pl.ds(al(c * HALF + 384 * (1 - inner), 128), 384)
    swap_q = [pltpu.make_async_remote_copy(
        src_ref=QT.at[:, :, third], dst_ref=AW.at[:, z, y, :, third], send_sem=ss.at[N_SITES],
        recv_sem=rs.at[N_SITES + at], device_id=dev(3 - lo, y, z, c), device_id_type=MESH,
    ) for at in (1 - inner, 0, 1)]
    swap_q[0].start()
    keep_q = pltpu.make_async_copy(QT.at[:, :, cols], mine_q, ls.at[6])

    @pl.when(hi == 0)
    def _():
        keep_q.start()

    swap_o = []
    for k, xx in enumerate((xp, xm)):
        sub = pl.ds(al(c * HALF + 384 * k, 128), 384)
        swap_o.append(st.go(out_in.at[:, sub], OW.at[lo, z, y, :, sub], dev(xx, y, z, c)))

    lastr, firstr = feat.at[pl.ds(496, 16)], feat.at[pl.ds(0, 16)]
    xn = m4(x + 2 * c)
    xq = m4(x + 2 * (1 - c))
    halo = [
        st.go(lastr, F.at[pl.ds(0, 16)], dev(xn, y, z, 1 - c)),
        st.go(firstr, F.at[pl.ds(528, 16)], dev(xq, y, z, 1 - c)),
        st.go(lastr, F.at[pl.ds(544, 16)], dev(m4(xn + 1), y, z, 1 - c)),
        st.go(firstr, F.at[pl.ds(1104, 16)], dev(m4(xq - 1), y, z, 1 - c)),
        st.go(feat.at[pl.ds(0, 272)], F.at[pl.ds(560, 272)], dev(xp, y, z, c)),
        st.go(feat.at[pl.ds(240, 272)], F.at[pl.ds(832, 272)], dev(xm, y, z, c)),
    ]

    acc[...] = jnp.zeros_like(acc)

    def ready_features():
        own_f.wait()
        own_o.wait()
        for cp in own_w:
            cp.wait()
        for cp in halo:
            cp.wait_recv()
        sa = 2 * lax.div(xm, 2) + c
        sbk = 2 * lax.div(xp, 2) + c
        for cond, at in ((s == 0, 0), (s == 3, 528), (sa == 0, 544), (sbk == 3, 1104)):
            @pl.when(cond)
            def _(at=at):
                F[at:at + 16] = jnp.zeros((16, D), BF)

    def wait_swap():
        @pl.when(hi == 0)
        def _():
            keep_q.wait()

        @pl.when(hi == 1)
        def _():
            swap_q[1].wait_recv()
            swap_q[2].wait_recv()

    def conv_tap(n, t):
        for k, (m, t0, t1) in enumerate(CHUNKS):
            if m == n and t0 <= t < t1 and sb[k]:
                for cp in sb[k]:
                    cp.wait_recv()
                sb[k] = []
        out = nt(F[...], CW[n, t])
        for j in range(2):
            acc[2 * n + j, 4 - t:4 - t + ROWS] += out[:, 128 * j:128 * j + 128]

    i0, k0 = (1 - c) * y + c * z, (1 - c) * z + c * y

    class Gather:
        def __init__(self, buf):
            self.buf = buf
            self.b1, self.a2, self.b2 = [], {}, {}

        def ref(self, i, k, sub=None):
            zz, yy = (1 - c) * k + c * i, (1 - c) * i + c * k
            if sub is None:
                return self.buf.at[:, zz, yy, :, cols]
            return self.buf.at[:, zz, yy, :, pl.ds(al(c * HALF + 384 * sub, 128), 384)]

        def to(self, i, k):
            return dev(x, (1 - c) * i + c * k, (1 - c) * k + c * i, c)

        def second(self, j):
            i = m4(i0 + j)
            own = self.ref(i, k0)
            self.a2[j] = [same(own, self.to(i0, m4(k0 + d))) for d in (1, -1)]

        def second_pass(self, j):
            i = m4(i0 + j)
            self.a2[j][0].wait_recv()
            self.b2[j] = [same(self.ref(i, m4(k0 - 1), 0), self.to(i0, m4(k0 + 1)))]
            self.a2[j][1].wait_recv()
            self.b2[j].append(same(self.ref(i, m4(k0 + 1), 1), self.to(i0, m4(k0 - 1))))

        def p0(self):
            own = self.ref(i0, k0)
            self.a1 = [same(own, self.to(m4(i0 + d), k0)) for d in (1, -1)]
            self.second(0)

        def p1(self, sign):
            if sign > 0:
                self.a1[0].wait_recv()
                self.b1.append(same(self.ref(m4(i0 - 1), k0, 0), self.to(m4(i0 + 1), k0)))
                self.second(-1)
            else:
                self.a1[1].wait_recv()
                self.b1.append(same(self.ref(m4(i0 + 1), k0, 1), self.to(m4(i0 - 1), k0)))
                self.second(1)

        def p2(self):
            for cp in self.b1:
                cp.wait_recv()
            self.second(2)

        def p5(self, js):
            for j in js:
                for cp in self.b2[j]:
                    cp.wait_recv()

        def to_sib(self, js):
            self.p5(js)
            for j in js:
                i = m4(i0 + j)
                a, b = self.buf.at[:, :, i, :, cols], self.buf.at[:, i, :, :, cols]
                to_core.append(st.either(c == 0, a, b, sib))

    gq, go = Gather(AW), Gather(OW)
    to_core = []

    s2 = 2 * (1 - hi) + c
    blk = pl.ds(al(s * 256, 256), 256)
    blk2 = pl.ds(al(s2 * 256, 256), 256)
    a0 = (2 * lax.div(xm, 2) + c) * 256
    b0 = (2 * lax.div(xp, 2) + c) * 256 + 128
    ids = id_in[...]
    lane = lax.broadcasted_iota(jnp.int32, (1, 8), 1)

    def piece(row, n):
        both = [VEC[row:row + 1, a * HALF + n * 256:a * HALF + n * 256 + 256] for a in range(2)]
        return jnp.where(jnp.full((1, 256), lo, jnp.int32) == 0, both[0], both[1])

    def tokens(at, window, n):
        kind = jnp.sum(jnp.where(lane == window, ids, 0), axis=1, keepdims=True)
        species = jnp.where(jnp.broadcast_to(kind, (1, 256)) == 0, piece(2, n), piece(3, n))
        bias = piece(0, n)
        cut = []
        for j in range(2):
            lanes = slice(128 * j, 128 * j + 128)
            even = jax.nn.gelu(acc[2 * n + j, pl.ds(at, 128, stride=2), :] + bias[:, lanes])
            odd = jax.nn.gelu(acc[2 * n + j, pl.ds(at + 1, 128, stride=2), :] + bias[:, lanes])
            cut.append((jnp.maximum(even, odd) + species[:, lanes]).astype(BF))
        return jnp.concatenate(cut, axis=1)

    cross, far, near = {}, {}, {}

    def send_tokens(n):
        wo = 2 * z + (1 - lo)
        TA[n, 0:128] = tokens(562, wo, n)
        TA[n, 128:256] = tokens(850, wo, n)
        ta, tb = TH.at[lo, n, pl.ds(al(a0, 128), 128)], TH.at[lo, n, pl.ds(al(b0, 128), 128)]
        cross[n] = []
        for xx in (xp, xm):
            cross[n] += [
                st.go(TA.at[n, pl.ds(0, 128)], ta, dev(xx, y, z, c)),
                st.go(TA.at[n, pl.ds(128, 128)], tb, dev(xx, y, z, c)),
            ]
        TH[lo, n, pl.ds(al(s * 256, 256), 128)] = tokens(18, p, n)
        TH[lo, n, pl.ds(al(s * 256 + 128, 128), 128)] = tokens(274, p, n)
        far[n] = same(TH.at[lo, n, blk], dev(x2, y, z, c))
        near[n] = [same(TH.at[lo, n, blk], sib)]

    def pass_cross(n):
        for cp in cross[n]:
            cp.wait_recv()
        near[n].append(same(TH.at[1 - lo, n, blk], sib))
        near[n].append(same(TH.at[1 - lo, n, blk2], sib))

    def pass_far(n):
        far[n].wait_recv()
        near[n].append(same(TH.at[lo, n, blk2], sib))

    def norm(block):
        at = pl.ds(al(block * 256, 256), 256)
        ms = 0.0
        for a in range(2):
            for n in range(3):
                h = TH[a, n, at].astype(F32)
                ms = ms + jnp.sum(h * h, axis=1, keepdims=True)
        r = lax.rsqrt(ms / D + 1e-05)
        for a in range(2):
            for n in range(3):
                lanes = slice(a * HALF + n * 256, a * HALF + n * 256 + 256)
                NM[at, lanes] = (TH[a, n, at].astype(F32) * r * VEC[1:2, lanes]).astype(BF)

    def start_gq():
        wait_swap()
        gq.p0()

    def start_go():
        for cp in swap_o:
            cp.wait_recv()
        go.p0()

    sq = []

    def finish_gq():
        gq.p5((0, -1, 1, 2))
        other = pl.ds(al(2 * (1 - c), 2), 2)
        sq.append(same(AW.at[:, other, :, :, cols], sib))

    def norms(k):
        if k == 0:
            norm(s)
            norm(s2)
            hs = {(a, n): TH[a, n, blk] for a in range(2) for n in range(3)}
            TOK[...] = jnp.concatenate(
                [hs[a, n][:, b * 64:(b + 1) * 64] for b in range(4) for a in range(2) for n in range(3)], axis=1
            )
        else:
            for n in range(3):
                for cp in near[n]:
                    cp.wait_recv()
            norm(2 * hi + 1 - c)
            norm(2 * (1 - hi) + 1 - c)

    heads = pl.ds(al(2 * c, 2), 2)

    def keys_values(k):
        if k == 0:
            sq[0].wait_recv()
        w = AW[1:3, heads].reshape(4 * HEAD, D)
        for b in (s, s2) if k == 0 else (2 * hi + 1 - c, 2 * (1 - hi) + 1 - c):
            at = pl.ds(al(b * 256, 256), 256)
            res = nt(NM[at], w).astype(BF)
            for h in range(4):
                QH[1 + h // 2, h % 2, at] = res[:, h * HEAD:(h + 1) * HEAD]

    scale = math.log2(math.e) / math.sqrt(HEAD)
    lop = lax.rem(lo + hi, 2)
    my_cols = pl.ds(al(c * 384, 128), 384)
    back = []
    dests = [(1 - hi, c, x2, c), (1 - hi, 1 - c, x2, 1 - c), (hi, 1 - c, x, 1 - c), (hi, c, None, None)]

    def attend(d):
        dhi, dc, dx, dcc = dests[d]
        at = pl.ds(al((2 * dhi + dc) * 256, 256), 256)
        res = nt(NM[at], AW[0, heads].reshape(2 * HEAD, D)).astype(BF)
        for h in range(2):
            QH[0, h, at] = res[:, h * HEAD:(h + 1) * HEAD]
        for h in range(2):
            sc = nt(QH[0, h, at], QH[1, h])
            e = jnp.exp2((sc - jnp.max(sc, axis=1, keepdims=True)) * scale)
            inv = 1.0 / jnp.sum(e, axis=1, keepdims=True)
            AO[d, h] = (nn(e.astype(BF), QH[2, h]) * inv).astype(BF)
        both = jnp.concatenate([AO[d, 0], AO[d, 1]], axis=1)
        if dx is None:
            AT[lop, :, my_cols] = both
        else:
            BO[d] = both
            back.append(st.go(BO.at[d], AT.at[lop, :, my_cols], dev(dx, y, z, dcc)))

    def project(k):
        if k == 0:
            for cp in to_core:
                cp.wait_recv()
            back[2].wait_recv()

            def body(n, carry):
                at = pl.ds(al(n * 256, 256), 256)
                MX[:, at] = TOK[:, at].astype(F32) + nn(AT[lop], OW[lop, :, :, :, at].reshape(HALF, 256))
                return carry
        else:
            for cp in back[:2]:
                cp.wait_recv()

            def body(n, carry):
                at = pl.ds(al(n * 256, 256), 256)
                mixed = nn(AT[1 - lop], OW[1 - lop, :, :, :, at].reshape(HALF, 256))
                seq_out[:, at] = (MX[:, at] + mixed).astype(BF)
                return carry
        lax.fori_loop(0, 6, body, 0)

    done = {
        "Z": lambda k: k == 0 or start_zA(k), "A": pass_zA, "B": pass_zB, "Y": pass_yA, "C": pass_yC,
        "F": lambda k: ready_features(), "T": conv_tap, "S": send_tokens, "X": pass_cross, "W": pass_far,
        "g0": start_gq, "g+": lambda: gq.p1(1), "g-": lambda: gq.p1(-1), "gb": gq.p2, "gP": gq.second_pass,
        "gQ": finish_gq,
        "o0": start_go, "o+": lambda: go.p1(1), "o-": lambda: go.p1(-1), "ob": go.p2, "oP": go.second_pass,
        "oQ": lambda j: go.to_sib((j,)),
        "N": norms, "V": keys_values, "D": attend, "O": project,
    }
    for what, *at in ORDER:
        if what == "O" and at[0] == 1:
            sent = len(st.all) - 3
            for cp in st.all[:sent]:
                cp.wait_send()
        done[what](*at)

    rows = jnp.sum(seq_out[...].astype(F32).reshape(16, POOL, D), axis=1) * (1.0 / POOL)
    unit = (rows * lax.rsqrt(jnp.mean(rows * rows, axis=1, keepdims=True) + 1e-05)).astype(BF)
    LW[...] = nn(unit, lw[...]).astype(BF)
    RW[...] = nn(unit, rw[...]).astype(BF).astype(F32)

    lefts = [st.go(LW, L.at[p], (s, lax.rem(p + d, 8), y)) for d in range(1, 8)]
    L[p] = LW[...]

    def right_copy(q, half):
        return pltpu.make_async_remote_copy(
            src_ref=RW.at[pl.ds(8 * half, 8)], dst_ref=R.at[p], send_sem=ssr.at[2 * q + half],
            recv_sem=rsr.at[p], device_id=(q, 2 * s + half, y), device_id_type=MESH,
        )

    for q in range(4):
        for half in range(2):
            me = jnp.logical_and(p == 2 * s + half, q == s)

            @pl.when(jnp.logical_not(me))
            def _(q=q, half=half):
                right_copy(q, half).start()

            @pl.when(me)
            def _(half=half):
                R[p] = RW[8 * half:8 * half + 8, :]

    for cp in lefts:
        cp.wait_recv()
    for w in range(8):
        @pl.when(jnp.logical_not(jnp.logical_and(inside, p == w)))
        def _(w=w):
            pltpu.make_async_remote_copy(
                src_ref=RW.at[pl.ds(0, 8)], dst_ref=R.at[w], send_sem=ssr.at[0],
                recv_sem=rsr.at[w], device_id=(s, p, y), device_id_type=MESH,
            ).wait_recv()

    outer = L[...].astype(F32)[:, :, None, :] * R[...][:, None, :, :]
    pair_out[...] = nn(outer.reshape(1024, 128).astype(BF), mix[...]).astype(BF)

    for cp in st.all[sent:]:
        cp.wait_send()
    swap_q[0].wait_send()
    for q in range(4):
        for half in range(2):
            @pl.when(jnp.logical_not(jnp.logical_and(p == 2 * s + half, q == s)))
            def _(q=q, half=half):
                right_copy(q, half).wait_send()


def local(
    features, conv_weight, conv_bias, species_table, species_id, norm_gain,
    qkv_weight, out_weight, left_weight, right_weight, mix_weight,
):
    any_ = pl.BlockSpec(memory_space=pl.ANY)
    vm = pl.BlockSpec(memory_space=pltpu.VMEM)
    seq_out, pair_map = pl.pallas_call(
        main_kernel,
        out_shape=(jax.ShapeDtypeStruct((256, D), BF), jax.ShapeDtypeStruct((1024, 128), BF)),
        in_specs=[any_] * 4 + [vm] * 7,
        out_specs=(vm, vm),
        scratch_shapes=[
            pltpu.VMEM((ROWS, D), BF),
            pltpu.VMEM((3, 5, 256, D), BF),
            pltpu.VMEM((6, ROWS + 8, 128), F32),
            pltpu.VMEM((3, 48, D), BF),
            pltpu.VMEM((3, 4, 4, 48, D), BF),
            pltpu.VMEM((2, 4, 4, 48, D), BF),
            pltpu.VMEM((2, 3, 1024, 256), BF),
            pltpu.VMEM((3, 256, 256), BF),
            pltpu.VMEM((256, D), BF),
            pltpu.VMEM((1024, D), BF),
            pltpu.VMEM((3, 2, 1024, HEAD), BF),
            pltpu.VMEM((4, 2, 256, HEAD), BF),
            pltpu.VMEM((2, 256, HALF), BF),
            pltpu.VMEM((3, 256, 384), BF),
            pltpu.VMEM((256, D), F32),
            pltpu.VMEM((4, D), F32),
            pltpu.VMEM((16, 128), BF),
            pltpu.VMEM((16, 128), F32),
            pltpu.VMEM((8, 16, 128), BF),
            pltpu.VMEM((8, 8, 128), F32),
            pltpu.SemaphoreType.DMA((N_SITES + 2,)),
            pltpu.SemaphoreType.DMA((N_SITES + 2,)),
            pltpu.SemaphoreType.DMA((7,)),
            pltpu.SemaphoreType.DMA((8,)),
            pltpu.SemaphoreType.DMA((8,)),
        ],
        compiler_params=pltpu.CompilerParams(
            collective_id=0, has_side_effects=True, vmem_limit_bytes=62 * 2**20
        ),
        name="window",
    )(
        features.reshape(512, D), conv_weight, qkv_weight, out_weight, conv_bias, norm_gain,
        species_table, species_id, left_weight, right_weight, mix_weight,
    )
    return seq_out[None, None], pair_map.reshape(1, 8, 16, 8, 128)


def solution(mesh):
    return jax.shard_map(
        local,
        mesh=mesh,
        in_specs=(
            P("dp", "pair", "seq", None),
            P(None, "pair", None),
            P(),
            P(),
            P("dp", None),
            P(),
            P(None, ("pair", "dp"), None),
            P(("pair", "dp"), None),
            P(),
            P(),
            P(),
        ),
        out_specs=(P("dp", "pair", "seq", None), P("dp", None, "seq", "pair", None)),
        check_vma=False,
    )
```

time: 114 us -> 106 us (0.930)
  Pallas kernels: 107 us -> 101 us
  local copies, waits for them, and re-layouts: 6.32 us -> 3.73 us
    pallas_call x1 -> x0, Pallas kernels: 8.16 us -> none  [local(): pl.pallas_call(pair_kernel, out_shape=jax.ShapeDtypeStruct((1024, 128), B...]
    broadcast_in_dim x2 -> x0, local copies, waits for them, and re-layouts: 2.59 us -> none  [the longest x1 1.3 us: local(): conv_bias[None]]
    pallas_call x1, Pallas kernels: 98.8 us -> 101 us  [local(): pl.pallas_call(main_kernel, out_shape=(jax.ShapeDtypeStruct((256, D), BF)...]
where the time goes in v3:
time: 106 us; the launch traced here: 105 us
  Pallas kernels  101 us (95%)
  local copies, waits for them, and re-layouts  3.73 us (4%)
    pallas_call x1, Pallas kernels, local(): pl.pallas_call(main_kernel, out_shape=(jax.ShapeDtypeStruct((256, D), BF)...  101 us
    unnamed x2, local copies, waits for them, and re-layouts  3.73 us

profile of v3, /device:TPU:1, one launch (start us, length us, event | category | flops | bytes accessed | tf_op | source)
XLA Modules:
  0.0 105.5 jit_solution(11452549397624160020)
XLA Ops:
  0.6 101.1 %window.1 = (bf16[256,1536]{1,0:T(8,128)(2,1)}, bf16[1024,128]{1,0:T(8,128)(2,1)}) custom-call(bf16[512,1536]{1,0:T(8,128)(2,1)} %bitcast.3, bf16[5,192,1536]{2,1,0:T(8,128)(2,1)} %cw_in.1, bf16[3,48,1536]{2,1,0:T(8,128)(2,1)} %qkv_in.1, bf16[48,1536]{1,0:T(8,128)(2,1)} %out_in.1, f32[1536]{0:T(1024)} %bias_in.1, f32[1536]{0:T(1024)} %gain_in.1, ...), custom_call_target="tpu_custom_call" | custom-call | tf_op jit(solution)/shard_map/window/pallas_call | solution.py:555
  101.8 2.1 %copy.15 = bf16[1,1,256,1536]{3,2,1,0:T(8,128)(2,1)} copy(bf16[1,1,256,1536]{3,2,1,0:T(8,128)(2,1)} %bitcast.4) | data formatting | bytes 1572864
  103.8 1.7 %copy.16 = bf16[1,8,16,8,128]{4,3,2,1,0:T(8,128)(2,1)} copy(bf16[1,8,16,8,128]{4,3,2,1,0:T(8,128)(2,1)} %bitcast.5) | data formatting | bytes 524288

commit v4 on v3

--- a/solution.py
+++ b/solution.py
@@ -88,10 +88,10 @@
     ("T", 0, 2), ("T", 0, 3), ("A", 8), ("g0",), ("T", 0, 4), ("B", 7), ("C", 6), ("Y", 7), ("S", 0),
     ("T", 1, 0), ("B", 8), ("Y", 8), ("T", 1, 1), ("T", 1, 2), ("T", 1, 3), ("T", 1, 4), ("g+",), ("g-",),
     ("gP", 0), ("S", 1), ("X", 0), ("W", 0), ("C", 7), ("T", 2, 0), ("C", 8), ("T", 2, 1), ("gP", -1),
-    ("T", 2, 2), ("gb",), ("T", 2, 3), ("T", 2, 4), ("gP", 1), ("S", 2), ("X", 1), ("W", 1), ("gP", 2),
-    ("o0",), ("X", 2), ("W", 2), ("gQ",), ("N", 0), ("o+",), ("o-",), ("oP", 0), ("N", 1), ("V", 0), ("V", 1),
-    ("ob",), ("oP", -1), ("D", 0), ("oP", 1), ("D", 1), ("oQ", 0), ("D", 2), ("oP", 2), ("D", 3), ("oQ", -1),
-    ("oQ", 1), ("oQ", 2), ("O", 0), ("O", 1),
+    ("T", 2, 2), ("gb",), ("o0",), ("T", 2, 3), ("T", 2, 4), ("gP", 1), ("S", 2), ("X", 1), ("W", 1),
+    ("gP", 2), ("o+",), ("o-",), ("X", 2), ("oP", 0), ("ob",), ("W", 2), ("gQ",), ("N", 0), ("N", 1),
+    ("V", 0), ("V", 1), ("D", 0), ("D", 1), ("oP", -1), ("oP", 1), ("oQ", 0), ("D", 2), ("oP", 2), ("D", 3),
+    ("oQ", -1), ("oQ", 1), ("oQ", 2), ("O", 0), ("O", 1),
 ]
 
 

time: 106 us -> 106 us (level)
  no operation moved by 1% of the time
where the time goes in v4:
time: 106 us
  Pallas kernels  101 us (95%)
  local copies, waits for them, and re-layouts  3.73 us (4%)
    pallas_call x1, Pallas kernels, local(): pl.pallas_call(main_kernel, out_shape=(jax.ShapeDtypeStruct((256, D), BF)...  101 us
    unnamed x2, local copies, waits for them, and re-layouts  3.73 us

profile of v4, /device:TPU:1, one launch (start us, length us, event | category | flops | bytes accessed | tf_op | source)
XLA Modules:
  0.0 105.8 jit_solution(17716710601379864414)
XLA Ops:
  0.6 101.4 %window.1 = (bf16[256,1536]{1,0:T(8,128)(2,1)}, bf16[1024,128]{1,0:T(8,128)(2,1)}) custom-call(bf16[512,1536]{1,0:T(8,128)(2,1)} %bitcast.3, bf16[5,192,1536]{2,1,0:T(8,128)(2,1)} %cw_in.1, bf16[3,48,1536]{2,1,0:T(8,128)(2,1)} %qkv_in.1, bf16[48,1536]{1,0:T(8,128)(2,1)} %out_in.1, f32[1536]{0:T(1024)} %bias_in.1, f32[1536]{0:T(1024)} %gain_in.1, ...), custom_call_target="tpu_custom_call" | custom-call | tf_op jit(solution)/shard_map/window/pallas_call | solution.py:555
  102.0 2.1 %copy.15 = bf16[1,1,256,1536]{3,2,1,0:T(8,128)(2,1)} copy(bf16[1,1,256,1536]{3,2,1,0:T(8,128)(2,1)} %bitcast.4) | data formatting | bytes 1572864
  104.1 1.7 %copy.16 = bf16[1,8,16,8,128]{4,3,2,1,0:T(8,128)(2,1)} copy(bf16[1,8,16,8,128]{4,3,2,1,0:T(8,128)(2,1)} %bitcast.5) | data formatting | bytes 524288
